TPU v7x, 32 devices: a whole 2x2x4 slice. The times are simulated.
32 devices in a mesh: section: 2 (over core), tensor: 2 (over x), dp: 8 (over z, y).
Axes of the slice: x: 2, y: 2, z: 4, core: 2. Of those that a mesh axis runs over, the one named last changes fastest.
Arguments:
- inputs: bfloat16 [16, 1024, 768], P('dp', 'tensor'), may hold values from -6 to 6
- segments: int32 [16, 1024], P('dp'), may hold values from 0 to 3, never falling along the last dimension, each value on 1 to 768 neighbouring positions
- cotangent: bfloat16 [16, 1024, 768], P('dp', 'tensor'), may hold values from -6 to 6
- norm_gains: bfloat16 [2, 2, 768], P('section'), may hold values from 0.5 to 1.5
- shared_biases: bfloat16 [2, 4, 768], P('section'), may hold values from -1.5 to 1.5
- w_qkv: bfloat16 [2, 768, 3, 768], P('section', None, None, 'tensor'), may hold values from -0.3125 to 0.3125
- qv_bias: bfloat16 [2, 2, 768], P('section', None, 'tensor'), may hold values from -1.5 to 1.5
- w_out: bfloat16 [2, 768, 768], P('section', 'tensor'), may hold values from -0.875 to 0.875
- w_up: bfloat16 [2, 768, 3072], P('section', None, 'tensor'), may hold values from -0.21875 to 0.21875
- up_bias: bfloat16 [2, 3072], P('section', 'tensor'), may hold values from -1.5 to 1.5
- w_down: bfloat16 [2, 3072, 768], P('section', 'tensor'), may hold values from -0.109375 to 0.109375
Outputs:
- activations: bfloat16 [2, 16, 1024, 768], P('section', 'dp', 'tensor')
- input_grads: bfloat16 [2, 16, 1024, 768], P('section', 'dp', 'tensor')
- grad_qkv: float32 [2, 768, 3, 768], P('section', None, None, 'tensor')
- grad_qv_bias: float32 [2, 2, 768], P('section', None, 'tensor')
- grad_out: float32 [2, 768, 768], P('section', 'tensor')
- grad_up: float32 [2, 768, 3072], P('section', None, 'tensor')
- grad_up_bias: float32 [2, 3072], P('section', 'tensor')
- grad_down: float32 [2, 3072, 768], P('section', 'tensor')
- grad_gains: float32 [2, 2, 768], P('section')
- grad_shifts: float32 [2, 4, 768], P('section')
Inputs may be any that keep to these rules, and one draw needn't show every extreme that they name: `segments`: each row's numbers never fall; a number's run is 1 to 768 tokens long, and one run of every row has exactly that length.
All inputs are finite; a program needn't handle non-finite values.
Results may differ from a plain program's by a relative error of at most 0.03.
Values may be sent and summed in bfloat16 or wider, within the bound.
A program may use at most 320 MiB of HBM per device.

v0:
```python
import jax
import jax.numpy as jnp
from jax import lax
from jax.sharding import PartitionSpec as P

HEAD = 64


eps_norm = 1e-05


def shifted(block, axis, distance):
    devices = range(lax.axis_size(axis))
    route = [(i - distance, i) for i in devices if i - distance in devices]
    return lax.ppermute(block, axis, route)


def smooth(values_in):
    return jax.nn.gelu(values_in, approximate=True)


def dot_rows(left, right):
    return lax.dot_general(
        left, right, (((0,), (0,)), ((), ())), preferred_element_type=jnp.float32
    )


def dot_last(left, right):
    return lax.dot_general(
        left, right, (((1,), (1,)), ((), ())), preferred_element_type=jnp.float32
    )


def norm_forward(rows_in, gain, shift):
    row_mean = jnp.mean(rows_in, axis=-1, keepdims=True)
    centred = rows_in - row_mean
    inv_dev = lax.rsqrt(jnp.mean(centred * centred, axis=-1, keepdims=True) + eps_norm)
    unit_rows = centred * inv_dev
    return (unit_rows * gain + shift, unit_rows, inv_dev)


def norm_backward(grad_out, unit_rows, inv_dev, gain):
    scaled = grad_out * gain
    grad_in = inv_dev * (
        scaled
        - jnp.mean(scaled, axis=-1, keepdims=True)
        - unit_rows * jnp.mean(scaled * unit_rows, axis=-1, keepdims=True)
    )
    return (grad_in, jnp.sum(grad_out * unit_rows, axis=0), jnp.sum(grad_out, axis=0))


def block_shape(seq_total):
    block_count = max(1, seq_total // 512)
    return (block_count, seq_total // block_count)


def allowed_block(begin_at, block_len, seg_ids):
    q_pos = begin_at + jnp.arange(block_len)
    k_pos = jnp.arange(seg_ids.shape[0])
    q_seg = seg_ids[begin_at : begin_at + block_len]
    return (k_pos[None, :] <= q_pos[:, None]) & (q_seg[:, None] == seg_ids[None, :])


def attention_forward(queries, key_rows, value_rows, seg_ids):
    block_count, block_len = block_shape(queries.shape[0])
    pieces, totals = ([], [])
    for block_no in range(block_count):
        begin_at = block_no * block_len
        scores = jnp.einsum(
            "qhd,khd->hqk",
            queries[begin_at : begin_at + block_len],
            key_rows,
            preferred_element_type=jnp.float32,
        )
        scores = jnp.where(allowed_block(begin_at, block_len, seg_ids)[None], scores, -1e30)
        row_top = jnp.max(scores, axis=-1, keepdims=True)
        weights = jnp.exp(scores - row_top)
        summed = jnp.sum(weights, axis=-1, keepdims=True)
        prob_rows = (weights / summed).astype(jnp.bfloat16)
        pieces.append(
            jnp.einsum("hqk,khd->qhd", prob_rows, value_rows, preferred_element_type=jnp.float32)
        )
        totals.append(row_top + jnp.log(summed))
    return (jnp.concatenate(pieces, axis=0), jnp.concatenate(totals, axis=1))


def attention_backward(queries, key_rows, value_rows, seg_ids, totals, grad_mixed):
    block_count, block_len = block_shape(queries.shape[0])
    grad_queries = []
    grad_keys = jnp.zeros(key_rows.shape, jnp.float32)
    grad_values = jnp.zeros(value_rows.shape, jnp.float32)
    for block_no in range(block_count):
        begin_at = block_no * block_len
        part_query = queries[begin_at : begin_at + block_len]
        part_grad = grad_mixed[begin_at : begin_at + block_len]
        scores = jnp.einsum(
            "qhd,khd->hqk", part_query, key_rows, preferred_element_type=jnp.float32
        )
        scores = jnp.where(allowed_block(begin_at, block_len, seg_ids)[None], scores, -1e30)
        prob_exact = jnp.exp(scores - totals[:, begin_at : begin_at + block_len])
        prob_rows = prob_exact.astype(jnp.bfloat16)
        grad_probs = jnp.einsum(
            "qhd,khd->hqk", part_grad, value_rows, preferred_element_type=jnp.float32
        )
        row_dot = jnp.sum(prob_exact * grad_probs, axis=-1, keepdims=True)
        grad_scores = (prob_exact * (grad_probs - row_dot)).astype(jnp.bfloat16)
        grad_queries.append(
            jnp.einsum("hqk,khd->qhd", grad_scores, key_rows, preferred_element_type=jnp.float32)
        )
        grad_keys = grad_keys + jnp.einsum(
            "hqk,qhd->khd", grad_scores, part_query, preferred_element_type=jnp.float32
        )
        grad_values = grad_values + jnp.einsum(
            "hqk,qhd->khd", prob_rows, part_grad, preferred_element_type=jnp.float32
        )
    return (jnp.concatenate(grad_queries, axis=0), grad_keys, grad_values)


def local(
    inputs,
    segments,
    cotangent,
    norm_gains,
    shared_biases,
    w_qkv,
    qv_bias,
    w_out,
    w_up,
    up_bias,
    w_down,
):
    is_first = lax.axis_index("section") == 0
    micro_count, half_rows, model_width = inputs.shape
    local_width = w_qkv.shape[3]
    head_count = local_width // HEAD
    q_scale = HEAD ** (-0.5)
    gain_rows = norm_gains[0].astype(jnp.float32)
    shifts = shared_biases[0].astype(jnp.float32)
    qkv_mat = w_qkv[0].reshape(model_width, 3 * local_width)
    qv_rows = qv_bias[0].astype(jnp.float32)
    out_mat = w_out[0]
    up_mat, down_mat, up_vec = (w_up[0], w_down[0], up_bias[0])
    up_shift = up_vec.astype(jnp.float32)
    zero_rows = jnp.zeros((half_rows, model_width), jnp.bfloat16)
    received = zero_rows
    outputs, kept_all = ([], [])
    for tick_no in range(micro_count + 1):
        own_micro = min(tick_no, micro_count - 1)
        prior_micro = max(tick_no - 1, 0)
        layer_in = jnp.where(is_first, inputs[own_micro], received).astype(jnp.float32)
        seg_ids = jnp.where(is_first, segments[own_micro], segments[prior_micro])
        normed, forward_unit1, forward_inv1 = norm_forward(layer_in, gain_rows[0], shifts[0])
        forward_normed_all = lax.all_gather(
            normed.astype(jnp.bfloat16), "tensor", axis=0, tiled=True
        )
        forward_seq_total = forward_normed_all.shape[0]
        projected = jnp.dot(
            forward_normed_all, qkv_mat, preferred_element_type=jnp.float32
        ).reshape(forward_seq_total, 3, local_width)
        forward_queries = (
            ((projected[:, 0] + qv_rows[0]) * q_scale)
            .astype(jnp.bfloat16)
            .reshape(forward_seq_total, head_count, HEAD)
        )
        forward_key_rows = (
            projected[:, 1].astype(jnp.bfloat16).reshape(forward_seq_total, head_count, HEAD)
        )
        forward_value_rows = (
            (projected[:, 2] + qv_rows[1])
            .astype(jnp.bfloat16)
            .reshape(forward_seq_total, head_count, HEAD)
        )
        forward_mixed_rows, forward_totals = attention_forward(
            forward_queries, forward_key_rows, forward_value_rows, seg_ids
        )
        forward_mixed_rows = forward_mixed_rows.reshape(forward_seq_total, local_width).astype(
            jnp.bfloat16
        )
        middle = (
            layer_in
            + lax.psum_scatter(
                jnp.dot(forward_mixed_rows, out_mat, preferred_element_type=jnp.float32).astype(
                    jnp.bfloat16
                ),
                "tensor",
                scatter_dimension=0,
                tiled=True,
            ).astype(jnp.float32)
            + shifts[2]
        )
        forward_normed2, forward_unit2, forward_inv2 = norm_forward(middle, gain_rows[1], shifts[1])
        forward_normed2 = forward_normed2.astype(jnp.bfloat16)
        forward_normed2 = lax.all_gather(forward_normed2, "tensor", axis=0, tiled=True)
        forward_hidden = (
            jnp.dot(forward_normed2, up_mat, preferred_element_type=jnp.float32) + up_shift
        )
        forward_active = smooth(forward_hidden).astype(jnp.bfloat16)
        branch2 = lax.psum_scatter(
            jnp.dot(forward_active, down_mat, preferred_element_type=jnp.float32).astype(
                jnp.bfloat16
            ),
            "tensor",
            scatter_dimension=0,
            tiled=True,
        ).astype(jnp.float32)
        output = (middle + branch2 + shifts[3]).astype(jnp.bfloat16)
        forward_kept_state = (
            seg_ids,
            forward_unit1,
            forward_inv1,
            forward_normed_all,
            forward_queries,
            forward_key_rows,
            forward_value_rows,
            forward_totals,
            forward_mixed_rows,
            forward_unit2,
            forward_inv2,
            forward_normed2,
            forward_hidden,
            forward_active,
        )
        output, kept_state = (output, forward_kept_state)
        outputs.append(output)
        kept_all.append(kept_state)
        if tick_no < micro_count:
            received = shifted(output, "section", 1)
    grad_sums = (
        jnp.zeros((model_width, 3 * local_width), jnp.float32),
        jnp.zeros((2, local_width), jnp.float32),
        jnp.zeros(out_mat.shape, jnp.float32),
        jnp.zeros(up_mat.shape, jnp.float32),
        jnp.zeros(up_vec.shape, jnp.float32),
        jnp.zeros(down_mat.shape, jnp.float32),
        jnp.zeros((2, model_width), jnp.float32),
        jnp.zeros((4, model_width), jnp.float32),
    )
    received = zero_rows
    grads_in = []
    for tick_no in range(micro_count + 1):
        kept_slot = micro_count - tick_no
        fresh_grad = cotangent[kept_slot - 1] if kept_slot >= 1 else zero_rows
        incoming = jnp.where(is_first, received, fresh_grad).astype(jnp.float32)
        (
            backward_seg_ids,
            unit1,
            inv1,
            normed_all,
            queries,
            key_rows,
            value_rows,
            totals,
            mixed_rows,
            unit2,
            inv2,
            normed2,
            hidden,
            active,
        ) = kept_all[kept_slot]
        (
            backward_g_qkv,
            backward_g_qv,
            backward_g_out,
            backward_g_up,
            backward_g_upb,
            backward_g_down,
            backward_g_gain,
            backward_g_shift,
        ) = grad_sums
        seq_total = normed_all.shape[0]
        grad_branch2 = incoming.astype(jnp.bfloat16)
        ignored, gelu_back = jax.vjp(smooth, hidden)
        grad_all = lax.all_gather(grad_branch2, "tensor", axis=0, tiled=True)
        grad_active = dot_last(grad_all, down_mat)
        backward_g_down = backward_g_down + dot_rows(active, grad_all)
        grad_hidden = gelu_back(grad_active)[0].astype(jnp.bfloat16)
        backward_g_up = backward_g_up + dot_rows(normed2, grad_hidden)
        backward_g_upb = backward_g_upb + jnp.sum(grad_hidden.astype(jnp.float32), axis=0)
        grad_normed2 = lax.psum_scatter(
            dot_last(grad_hidden, up_mat).astype(jnp.bfloat16),
            "tensor",
            scatter_dimension=0,
            tiled=True,
        ).astype(jnp.float32)
        norm2_grad, gain2, shift2 = norm_backward(grad_normed2, unit2, inv2, gain_rows[1])
        grad_middle = incoming + norm2_grad
        grad_branch = grad_middle.astype(jnp.bfloat16)
        grad_branch_all = lax.all_gather(grad_branch, "tensor", axis=0, tiled=True)
        backward_g_out = backward_g_out + dot_rows(mixed_rows, grad_branch_all)
        grad_mixed = (
            dot_last(grad_branch_all, out_mat)
            .astype(jnp.bfloat16)
            .reshape(seq_total, head_count, HEAD)
        )
        grad_queries, grad_keys, grad_values = attention_backward(
            queries, key_rows, value_rows, backward_seg_ids, totals, grad_mixed
        )
        grad_queries = (grad_queries * q_scale).astype(jnp.bfloat16).reshape(seq_total, local_width)
        grad_keys = grad_keys.astype(jnp.bfloat16).reshape(seq_total, local_width)
        grad_values = grad_values.astype(jnp.bfloat16).reshape(seq_total, local_width)
        grad_proj = jnp.concatenate([grad_queries, grad_keys, grad_values], axis=1)
        backward_g_qkv = backward_g_qkv + dot_rows(normed_all, grad_proj)
        backward_g_qv = backward_g_qv + jnp.stack(
            [
                jnp.sum(grad_queries.astype(jnp.float32), axis=0),
                jnp.sum(grad_values.astype(jnp.float32), axis=0),
            ]
        )
        grad_normed = lax.psum_scatter(
            dot_last(grad_proj, qkv_mat).astype(jnp.bfloat16),
            "tensor",
            scatter_dimension=0,
            tiled=True,
        ).astype(jnp.float32)
        norm1_grad, gain1, shift1 = norm_backward(grad_normed, unit1, inv1, gain_rows[0])
        grad_in = grad_middle + norm1_grad
        backward_g_gain = backward_g_gain + jnp.stack([gain1, gain2])
        backward_g_shift = backward_g_shift + jnp.stack(
            [
                shift1,
                shift2,
                jnp.sum(grad_branch.astype(jnp.float32), axis=0),
                jnp.sum(grad_branch2.astype(jnp.float32), axis=0),
            ]
        )
        grad_in, grad_sums = (
            grad_in.astype(jnp.bfloat16),
            (
                backward_g_qkv,
                backward_g_qv,
                backward_g_out,
                backward_g_up,
                backward_g_upb,
                backward_g_down,
                backward_g_gain,
                backward_g_shift,
            ),
        )
        grads_in.append(grad_in)
        if tick_no < micro_count:
            received = shifted(grad_in, "section", -1)
    act_rows = jnp.stack(
        [
            jnp.where(is_first, outputs[index_no], outputs[index_no + 1])
            for index_no in range(micro_count)
        ]
    )
    grad_rows_out = jnp.stack(
        [
            jnp.where(
                is_first, grads_in[micro_count - index_no], grads_in[micro_count - 1 - index_no]
            )
            for index_no in range(micro_count)
        ]
    )
    g_qkv, g_qv, g_out, g_up, g_upb, g_down, g_gain, g_shift = grad_sums
    g_qkv, g_qv, g_out, g_up, g_upb, g_down = lax.psum(
        (g_qkv, g_qv, g_out, g_up, g_upb, g_down), "dp"
    )
    g_gain, g_shift = lax.psum((g_gain, g_shift), ("tensor", "dp"))
    return (
        act_rows[None],
        grad_rows_out[None],
        g_qkv.reshape(model_width, 3, local_width)[None],
        g_qv[None],
        g_out[None],
        g_up[None],
        g_upb[None],
        g_down[None],
        g_gain[None],
        g_shift[None],
    )


def solution(mesh):
    return jax.shard_map(
        local,
        mesh=mesh,
        in_specs=(
            P("dp", "tensor", None),
            P("dp", None),
            P("dp", "tensor", None),
            P("section", None, None),
            P("section", None, None),
            P("section", None, None, "tensor"),
            P("section", None, "tensor"),
            P("section", "tensor", None),
            P("section", None, "tensor"),
            P("section", "tensor"),
            P("section", "tensor", None),
        ),
        out_specs=(
            P("section", "dp", "tensor", None),
            P("section", "dp", "tensor", None),
            P("section", None, None, "tensor"),
            P("section", None, "tensor"),
            P("section", "tensor", None),
            P("section", None, "tensor"),
            P("section", "tensor"),
            P("section", "tensor", None),
            P("section", None, None),
            P("section", None, None),
        ),
        check_vma=False,
    )
```

profile of v0, /device:TPU:0, one launch (start us, length us, event | category | flops | bytes accessed | tf_op | source)
XLA Modules:
  0.0 1564.0 jit_solution(2588667289465846196)
XLA Ops:
  20.0 24.2 %all-gather.14.cloned.1.call-done = bf16[1024,768]{1,0:T(8,128)(2,1)} async-done(((bf16[512,768]{1,0:T(8,128)(2,1)}), bf16[1024,768]{1,0:T(8,128)(2,1)}) %all-gather.14.cloned.1.call-update) | async-done | bytes 1572880 | tf_op jit(solution)/shard_map/all_gather | solution.py:153
  76.7 26.0 %reduce-scatter.13.cloned.1.call-done = bf16[512,768]{1,0:T(8,128)(2,1)} async-done(((bf16[1024,768]{1,0:T(8,128)(2,1)}), bf16[512,768]{1,0:T(8,128)(2,1)}) %reduce-scatter.13.cloned.1.call-update) | async-done | bytes 786448 | tf_op jit(solution)/shard_map/reduce_scatter | solution.py:181
  108.1 27.3 %all-gather.16.cloned.1.call-done = bf16[1024,768]{1,0:T(8,128)(2,1)} async-done(((bf16[512,768]{1,0:T(8,128)(2,1)}), bf16[1024,768]{1,0:T(8,128)(2,1)}) %all-gather.16.cloned.1.call-update) | async-done | bytes 1572880 | tf_op jit(solution)/shard_map/all_gather | solution.py:193
  147.2 26.2 %reduce-scatter.15.cloned.1.call-done = bf16[512,768]{1,0:T(8,128)(2,1)} async-done(((bf16[1024,768]{1,0:T(8,128)(2,1)}), bf16[512,768]{1,0:T(8,128)(2,1)}) %reduce-scatter.15.cloned.1.call-update) | async-done | bytes 786448 | tf_op jit(solution)/shard_map/reduce_scatter | solution.py:198
  182.9 25.4 %all-gather.18.cloned.1.call-done = bf16[1024,768]{1,0:T(8,128)(2,1)} async-done(((bf16[512,768]{1,0:T(8,128)(2,1)}), bf16[1024,768]{1,0:T(8,128)(2,1)}) %all-gather.18.cloned.1.call-update) | async-done | bytes 1572880 | tf_op jit(solution)/shard_map/all_gather | solution.py:153
  239.0 25.8 %reduce-scatter.17.cloned.1.call-done = bf16[512,768]{1,0:T(8,128)(2,1)} async-done(((bf16[1024,768]{1,0:T(8,128)(2,1)}), bf16[512,768]{1,0:T(8,128)(2,1)}) %reduce-scatter.17.cloned.1.call-update) | async-done | bytes 786448 | tf_op jit(solution)/shard_map/reduce_scatter | solution.py:181
  269.4 27.3 %all-gather.20.cloned.1.call-done = bf16[1024,768]{1,0:T(8,128)(2,1)} async-done(((bf16[512,768]{1,0:T(8,128)(2,1)}), bf16[1024,768]{1,0:T(8,128)(2,1)}) %all-gather.20.cloned.1.call-update) | async-done | bytes 1572880 | tf_op jit(solution)/shard_map/all_gather | solution.py:193
  309.0 26.2 %reduce-scatter.19.cloned.1.call-done = bf16[512,768]{1,0:T(8,128)(2,1)} async-done(((bf16[1024,768]{1,0:T(8,128)(2,1)}), bf16[512,768]{1,0:T(8,128)(2,1)}) %reduce-scatter.19.cloned.1.call-update) | async-done | bytes 786448 | tf_op jit(solution)/shard_map/reduce_scatter | solution.py:198
  345.9 25.4 %all-gather.22.cloned.1.call-done = bf16[1024,768]{1,0:T(8,128)(2,1)} async-done(((bf16[512,768]{1,0:T(8,128)(2,1)}), bf16[1024,768]{1,0:T(8,128)(2,1)}) %all-gather.22.cloned.1.call-update) | async-done | bytes 1572880 | tf_op jit(solution)/shard_map/all_gather | solution.py:153
  402.3 26.0 %reduce-scatter.21.cloned.1.call-done = bf16[512,768]{1,0:T(8,128)(2,1)} async-done(((bf16[1024,768]{1,0:T(8,128)(2,1)}), bf16[512,768]{1,0:T(8,128)(2,1)}) %reduce-scatter.21.cloned.1.call-update) | async-done | bytes 786448 | tf_op jit(solution)/shard_map/reduce_scatter | solution.py:181
  436.3 24.5 %all-gather.24.cloned.1.call-done = bf16[1024,768]{1,0:T(8,128)(2,1)} async-done(((bf16[512,768]{1,0:T(8,128)(2,1)}), bf16[1024,768]{1,0:T(8,128)(2,1)}) %all-gather.24.cloned.1.call-update) | async-done | bytes 1572880 | tf_op jit(solution)/shard_map/all_gather | solution.py:193
  466.7 23.4 %all-gather.36.cloned.1.call-done = bf16[1,1024,768]{2,1,0:T(8,128)(2,1)} async-done(((bf16[1,512,768]{2,1,0:T(8,128)(2,1)}), bf16[1,1024,768]{2,1,0:T(8,128)(2,1)}) %all-gather.36.cloned.1.call-update) | async-done | bytes 1572880 | tf_op jit(solution)/shard_map/all_gather | solution.py:273
  505.0 26.2 %reduce-scatter.25.cloned.1.call-done = bf16[512,768]{1,0:T(8,128)(2,1)} async-done(((bf16[1024,768]{1,0:T(8,128)(2,1)}), bf16[512,768]{1,0:T(8,128)(2,1)}) %reduce-scatter.25.cloned.1.call-update) | async-done | bytes 786448 | tf_op jit(solution)/shard_map/reduce_scatter | solution.py:279
  540.6 24.6 %all-gather.26.cloned.1.call-done = bf16[1024,768]{1,0:T(8,128)(2,1)} async-done(((bf16[512,768]{1,0:T(8,128)(2,1)}), bf16[1024,768]{1,0:T(8,128)(2,1)}) %all-gather.26.cloned.1.call-update) | async-done | bytes 1572880 | tf_op jit(solution)/shard_map/all_gather | solution.py:288
  568.5 11.5 multiply_reduce_fusion.5
  611.8 10.1 multiply_convert_fusion.4
  630.4 26.2 %reduce-scatter.27.cloned.1.call-done = bf16[512,768]{1,0:T(8,128)(2,1)} async-done(((bf16[1024,768]{1,0:T(8,128)(2,1)}), bf16[512,768]{1,0:T(8,128)(2,1)}) %reduce-scatter.27.cloned.1.call-update) | async-done | bytes 786448 | tf_op jit(solution)/shard_map/reduce_scatter | solution.py:309
  668.1 27.3 %all-gather.28.cloned.1.call-done = bf16[1024,768]{1,0:T(8,128)(2,1)} async-done(((bf16[512,768]{1,0:T(8,128)(2,1)}), bf16[1024,768]{1,0:T(8,128)(2,1)}) %all-gather.28.cloned.1.call-update) | async-done | bytes 1572880 | tf_op jit(solution)/shard_map/all_gather | solution.py:273
  710.5 26.0 %reduce-scatter.29.cloned.1.call-done = bf16[512,768]{1,0:T(8,128)(2,1)} async-done(((bf16[1024,768]{1,0:T(8,128)(2,1)}), bf16[512,768]{1,0:T(8,128)(2,1)}) %reduce-scatter.29.cloned.1.call-update) | async-done | bytes 786448 | tf_op jit(solution)/shard_map/reduce_scatter | solution.py:279
  743.8 26.1 %all-gather.30.cloned.1.call-done = bf16[1024,768]{1,0:T(8,128)(2,1)} async-done(((bf16[512,768]{1,0:T(8,128)(2,1)}), bf16[1024,768]{1,0:T(8,128)(2,1)}) %all-gather.30.cloned.1.call-update) | async-done | bytes 1572880 | tf_op jit(solution)/shard_map/all_gather | solution.py:288
  773.2 11.2 multiply_reduce_fusion.3
  816.3 10.0 multiply_convert_fusion.2
  834.8 26.2 %reduce-scatter.31.cloned.1.call-done = bf16[512,768]{1,0:T(8,128)(2,1)} async-done(((bf16[1024,768]{1,0:T(8,128)(2,1)}), bf16[512,768]{1,0:T(8,128)(2,1)}) %reduce-scatter.31.cloned.1.call-update) | async-done | bytes 786448 | tf_op jit(solution)/shard_map/reduce_scatter | solution.py:309
  873.4 27.3 %all-gather.32.cloned.1.call-done = bf16[1024,768]{1,0:T(8,128)(2,1)} async-done(((bf16[512,768]{1,0:T(8,128)(2,1)}), bf16[1024,768]{1,0:T(8,128)(2,1)}) %all-gather.32.cloned.1.call-update) | async-done | bytes 1572880 | tf_op jit(solution)/shard_map/all_gather | solution.py:273
  916.4 25.4 %reduce-scatter.33.cloned.1.call-done = bf16[512,768]{1,0:T(8,128)(2,1)} async-done(((bf16[1024,768]{1,0:T(8,128)(2,1)}), bf16[512,768]{1,0:T(8,128)(2,1)}) %reduce-scatter.33.cloned.1.call-update) | async-done | bytes 786448 | tf_op jit(solution)/shard_map/reduce_scatter | solution.py:279
  999.0 11.6 multiply_reduce_fusion.1
  1029.7 12.2 multiply_convert_fusion
  1065.7 10.2 add_bitcast_fusion.1
  1075.9 12.0 add_bitcast_fusion
  1106.1 23.8 %all-reduce.1 = (f32[1,2,384]{2,1,0:T(2,128)}, f32[1,1536]{1,0:T(1,128)}) all-reduce(f32[1,2,384]{2,1,0:T(2,128)S(1)} %fusion.263, f32[1,1536]{1,0:T(1,128)S(1)} %broadcast_in_dim.102), channel_id=1, replica_groups=mesh['section'=2,'tensor'=2,'dp'=8] {'dp'}, use_global_device_ids=true, to_apply=%region_61.62 | all-reduce | flops 2304 | bytes 18432 | tf_op jit(solution)/shard_map/psum | solution.py:357
  1132.2 76.4 %all-reduce = (f32[1,2,768]{2,1,0:T(2,128)}, f32[1,4,768]{2,1,0:T(4,128)}) all-reduce(f32[1,2,768]{2,1,0:T(2,128)S(1)} %fusion.261, f32[1,4,768]{2,1,0:T(4,128)S(1)} %fusion.259), channel_id=1, replica_groups=mesh['section'=2,'tensor'=2,'dp'=8] {'tensor','dp'}, use_global_device_ids=true, to_apply=%region_75.76 | all-reduce | flops 4608 | bytes 36864 | tf_op jit(solution)/shard_map/psum | solution.py:360
  1212.6 330.6 %all-reduce.5.cloned.1.call-done = (f32[1,768,3,384]{1,3,2,0:T(8,128)}, f32[1,384,768]{2,1,0:T(8,128)}, f32[1,768,1536]{2,1,0:T(8,128)}, f32[1,1536,768]{2,1,0:T(8,128)}) async-done(((f32[1,768,3,384]{1,3,2,0:T(8,128)}, f32[1,384,768]{2,1,0:T(8,128)}, f32[1,768,1536]{2,1,0:T(8,128)}, f32[1,1536,768]{2,1,0:T(8,128)}), (f32[1,768,3,384]{1,3,2,0:T(8,128)}, f32[1,384,768]{2,1,0:T(8,128)}, ...) | async-done | bytes 14155792 | tf_op jit(solution)/shard_map/psum | solution.py:357
  (775 shorter events, 484.2 us)
Async XLA Ops:
  7.2 37.1 %all-gather.14.cloned.1.call-start = ((), (), s32[]{:S(2)}) async-start(), calls=%async_computation.12 | async-start | bytes 2359296 | tf_op jit(solution)/shard_map/all_gather | solution.py:153
  11.8 852.0 %copy-start.110 = (f32[768]{0:T(1024)}, f32[768]{0:T(1024)S(1)}, u32[]{:S(2)}) copy-start(f32[768]{0:T(1024)S(1)} %get-tuple-element.155) | copy-start | bytes 9220
  14.2 88.5 %reduce-scatter.13.cloned.1.call-start = ((), (), s32[]{:S(2)}) async-start(), calls=%async_computation.13 | async-start | bytes 2359296 | tf_op jit(solution)/shard_map/reduce_scatter | solution.py:181
  14.3 198.2 %copy-start.180 = (f32[384]{0:T(512)}, f32[384]{0:T(512)S(1)}, u32[]{:S(2)}) copy-start(f32[384]{0:T(512)S(1)} %get-tuple-element.50) | copy-start | bytes 4612
  76.5 58.9 %all-gather.16.cloned.1.call-start = ((), (), s32[]{:S(2)}) async-start(), calls=%async_computation.14 | async-start | bytes 2359296 | tf_op jit(solution)/shard_map/all_gather | solution.py:193
  108.0 65.3 %reduce-scatter.15.cloned.1.call-start = ((), (), s32[]{:S(2)}) async-start(), calls=%async_computation.15 | async-start | bytes 2359296 | tf_op jit(solution)/shard_map/reduce_scatter | solution.py:198
  147.1 61.2 %all-gather.18.cloned.1.call-start = ((), (), s32[]{:S(2)}) async-start(), calls=%async_computation.16 | async-start | bytes 2359296 | tf_op jit(solution)/shard_map/all_gather | solution.py:153
  175.3 3.6 collective-permute-start
  180.9 83.9 %reduce-scatter.17.cloned.1.call-start = ((), (), s32[]{:S(2)}) async-start(), calls=%async_computation.17 | async-start | bytes 2359296 | tf_op jit(solution)/shard_map/reduce_scatter | solution.py:181
  238.6 58.2 %all-gather.20.cloned.1.call-start = ((), (), s32[]{:S(2)}) async-start(), calls=%async_computation.18 | async-start | bytes 2359296 | tf_op jit(solution)/shard_map/all_gather | solution.py:193
  269.4 65.8 %reduce-scatter.19.cloned.1.call-start = ((), (), s32[]{:S(2)}) async-start(), calls=%async_computation.19 | async-start | bytes 2359296 | tf_op jit(solution)/shard_map/reduce_scatter | solution.py:198
  309.0 62.4 %all-gather.22.cloned.1.call-start = ((), (), s32[]{:S(2)}) async-start(), calls=%async_computation.20 | async-start | bytes 2359296 | tf_op jit(solution)/shard_map/all_gather | solution.py:153
  338.4 3.5 collective-permute-start.1
  342.3 317.0 %copy-start.7 = (bf16[512,768]{1,0:T(8,128)(2,1)}, bf16[512,768]{1,0:T(8,128)(2,1)S(1)}, u32[]{:S(2)}) copy-start(bf16[512,768]{1,0:T(8,128)(2,1)S(1)} %get-tuple-element.86) | copy-start | bytes 2359300
  344.0 84.4 %reduce-scatter.21.cloned.1.call-start = ((), (), s32[]{:S(2)}) async-start(), calls=%async_computation.21 | async-start | bytes 2359296 | tf_op jit(solution)/shard_map/reduce_scatter | solution.py:181
  402.1 58.7 %all-gather.24.cloned.1.call-start = ((), (), s32[]{:S(2)}) async-start(), calls=%async_computation.22 | async-start | bytes 2359296 | tf_op jit(solution)/shard_map/all_gather | solution.py:193
  433.4 56.7 %all-gather.36.cloned.1.call-start = ((), (), s32[]{:S(2)}) async-start(), calls=%async_computation.35 | async-start | bytes 2359296 | tf_op jit(solution)/shard_map/all_gather | solution.py:273
  436.3 94.9 %reduce-scatter.25.cloned.1.call-start = ((), (), s32[]{:S(2)}) async-start(), calls=%async_computation.24 | async-start | bytes 2359296 | tf_op jit(solution)/shard_map/reduce_scatter | solution.py:279
  505.0 60.3 %all-gather.26.cloned.1.call-start = ((), (), s32[]{:S(2)}) async-start(), calls=%async_computation.25 | async-start | bytes 2359296 | tf_op jit(solution)/shard_map/all_gather | solution.py:288
  537.9 118.7 %reduce-scatter.27.cloned.1.call-start = ((), (), s32[]{:S(2)}) async-start(), calls=%async_computation.26 | async-start | bytes 2359296 | tf_op jit(solution)/shard_map/reduce_scatter | solution.py:309
  630.3 65.1 %all-gather.28.cloned.1.call-start = ((), (), s32[]{:S(2)}) async-start(), calls=%async_computation.27 | async-start | bytes 2359296 | tf_op jit(solution)/shard_map/all_gather | solution.py:273
  662.0 4.3 collective-permute-start.2
  668.1 68.4 %reduce-scatter.29.cloned.1.call-start = ((), (), s32[]{:S(2)}) async-start(), calls=%async_computation.28 | async-start | bytes 2359296 | tf_op jit(solution)/shard_map/reduce_scatter | solution.py:279
  710.3 59.6 %all-gather.30.cloned.1.call-start = ((), (), s32[]{:S(2)}) async-start(), calls=%async_computation.29 | async-start | bytes 2359296 | tf_op jit(solution)/shard_map/all_gather | solution.py:288
  742.5 118.5 %reduce-scatter.31.cloned.1.call-start = ((), (), s32[]{:S(2)}) async-start(), calls=%async_computation.30 | async-start | bytes 2359296 | tf_op jit(solution)/shard_map/reduce_scatter | solution.py:309
  834.8 65.9 %all-gather.32.cloned.1.call-start = ((), (), s32[]{:S(2)}) async-start(), calls=%async_computation.31 | async-start | bytes 2359296 | tf_op jit(solution)/shard_map/all_gather | solution.py:273
  867.5 4.2 collective-permute-start.3
  873.3 68.5 %reduce-scatter.33.cloned.1.call-start = ((), (), s32[]{:S(2)}) async-start(), calls=%async_computation.32 | async-start | bytes 2359296 | tf_op jit(solution)/shard_map/reduce_scatter | solution.py:279
  915.5 80.9 %all-gather.34.cloned.1.call-start = ((), (), s32[]{:S(2)}) async-start(), calls=%async_computation.33 | async-start | bytes 2359296 | tf_op jit(solution)/shard_map/all_gather | solution.py:288
  949.1 152.4 %reduce-scatter.23.cloned.1.call-start = ((), (), s32[]{:S(2)}) async-start(), calls=%async_computation.23 | async-start | bytes 2359296 | tf_op jit(solution)/shard_map/reduce_scatter | solution.py:198
  962.9 166.9 %reduce-scatter.35.cloned.1.call-start = ((), (), s32[]{:S(2)}) async-start(), calls=%async_computation.34 | async-start | bytes 2359296 | tf_op jit(solution)/shard_map/reduce_scatter | solution.py:309
  1065.6 477.7 %all-reduce.5.cloned.1.call-start = ((), (), s32[]{:S(2)}) async-start(), calls=%async_computation.36 | async-start | bytes 28311552 | tf_op jit(solution)/shard_map/psum | solution.py:357
  (243 other events, 3039.0 us)
Sparse Core Ops, SparseCore 0:
  14.3 29.8 all-gather.13
  76.6 26.0 reduce-scatter.12
  108.1 27.2 all-gather.15
  147.2 26.0 reduce-scatter.14
  181.1 27.2 all-gather.17
  238.7 26.0 reduce-scatter.16
  269.5 27.2 all-gather.19
  309.1 26.0 reduce-scatter.18
  344.1 27.2 all-gather.21
  402.2 26.0 reduce-scatter.20
  433.6 27.2 all-gather.23
  462.8 27.1 all-gather.35
  505.1 26.0 reduce-scatter.24
  538.0 27.2 all-gather.25
  630.4 26.0 reduce-scatter.26
  668.2 27.2 all-gather.27
  710.4 26.0 reduce-scatter.28
  742.6 27.2 all-gather.29
  834.9 26.0 reduce-scatter.30
  873.4 27.2 all-gather.31
  915.7 26.0 reduce-scatter.32
  949.2 27.2 all-gather.33
  979.2 26.0 reduce-scatter.22
  1065.7 26.1 reduce-scatter.34
  1100.8 442.3 all-reduce.4
where the time goes:
time: 1570 us; the launch traced here: 1560 us
  waiting for transfers between devices  883 us (56%)
  matrix products  325 us (21%)
  other arithmetic  167 us (11%)
  blocking collectives  100 us (6%)
  local copies, waits for them, and re-layouts  62.7 us (4%)
  between operations  17.2 us (1%)
    psum x1, waiting for transfers between devices, local(): lax.psum((g_qkv, g_qv, g_out, g_up, g_upb, g_down), 'dp')  331 us
    all_gather x3, waiting for transfers between devices, local(): lax.all_gather(forward_normed2, 'tensor', axis=0, tiled=True)  79 us
    all_gather x3, waiting for transfers between devices, local(): grad_all = lax.all_gather(grad_branch2, 'tensor', axis=0, tiled=True)  78 us
    reduce_scatter x3, waiting for transfers between devices, local(): lax.psum_scatter(jnp.dot(forward_mixed_rows, out_mat, preferred_element_t...  77.8 us
    reduce_scatter x3, waiting for transfers between devices, local(): lax.psum_scatter(dot_last(grad_hidden, up_mat).astype(jnp.bfloat16), 'ten...  77.6 us
    psum x1, blocking collectives, local(): g_gain, g_shift = lax.psum((g_gain, g_shift), ('tensor', 'dp'))  76.4 us
    all_gather x3, waiting for transfers between devices, local(): lax.all_gather(normed.astype(jnp.bfloat16), 'tensor', axis=0, tiled=True)  75.1 us
    dot_general x6, matrix products, attention_backward(): jnp.einsum('qhd,khd->hqk', part_grad, value_rows, preferred_element_type=...  63 us
  transfers between devices with their start and end apart: 29, of which 26 were waited for; matrix products, arithmetic and copies ran while one was open for 11% of the time, Pallas kernels for 0%

commit v1 on v0

v1 whole, which is shorter than its diff:
```python
import jax
import jax.numpy as jnp
from jax import lax
from jax.sharding import PartitionSpec as P

HEAD = 64


eps_norm = 1e-05


GROUP = ("section", "tensor")


def flip(block, axis):
    return lax.ppermute(block, axis, [(0, 1), (1, 0)])


def spread(layer, block):
    near = lax.ppermute(block, GROUP, [(layer * 2 + t, t * 2 + t) for t in range(2)])
    far = lax.ppermute(block, GROUP, [(layer * 2 + t, t * 2 + 1 - t) for t in range(2)])
    return jnp.where(lax.axis_index("section") == lax.axis_index("tensor"), near, far)


def pair_sum(partial):
    part = partial.astype(jnp.bfloat16)
    return part.astype(jnp.float32) + flip(part, "section").astype(jnp.float32)


def collect(grad):
    x = lax.axis_index("tensor")
    rows = grad.shape[0] // 2
    low = grad.astype(jnp.bfloat16)
    first, second = low[:rows], low[rows:]
    same = jnp.where(x == 0, first, second)
    other = jnp.where(x == 0, second, first)
    a = lax.ppermute(same, GROUP, [(c * 2 + x, x * 2 + c) for c in range(2) for x in range(2)])
    b = lax.ppermute(
        other, GROUP, [(c * 2 + x, (1 - x) * 2 + c) for c in range(2) for x in range(2)]
    )
    return (a.astype(jnp.float32) + b.astype(jnp.float32)).astype(jnp.bfloat16)


def whole_rows(halves):
    x = lax.axis_index("tensor")
    own = jnp.where(x == 0, halves[0], halves[1])
    away = flip(jnp.where(x == 0, halves[1], halves[0]), "tensor")
    return jnp.concatenate([jnp.where(x == 0, own, away), jnp.where(x == 0, away, own)], axis=0)


def placed_rows(of_layers):
    s, x = lax.axis_index("section"), lax.axis_index("tensor")
    rows = jnp.where(s == 0, of_layers[0], of_layers[1])
    half = rows.shape[0] // 2
    first, second = rows[:half], rows[half:]
    keep = jnp.where(x == 0, first, second)
    away = flip(jnp.where(x == 0, second, first), "tensor")
    return jnp.stack([jnp.where(x == 0, keep, away), jnp.where(x == 0, away, keep)])[None]


def smooth(values_in):
    return jax.nn.gelu(values_in, approximate=True)


def dot_rows(left, right):
    return lax.dot_general(
        left, right, (((0,), (0,)), ((), ())), preferred_element_type=jnp.float32
    )


def dot_last(left, right):
    return lax.dot_general(
        left, right, (((1,), (1,)), ((), ())), preferred_element_type=jnp.float32
    )


def norm_forward(rows_in, gain, shift):
    row_mean = jnp.mean(rows_in, axis=-1, keepdims=True)
    centred = rows_in - row_mean
    inv_dev = lax.rsqrt(jnp.mean(centred * centred, axis=-1, keepdims=True) + eps_norm)
    unit_rows = centred * inv_dev
    return (unit_rows * gain + shift, unit_rows, inv_dev)


def norm_backward(grad_out, unit_rows, inv_dev, gain):
    scaled = grad_out * gain
    grad_in = inv_dev * (
        scaled
        - jnp.mean(scaled, axis=-1, keepdims=True)
        - unit_rows * jnp.mean(scaled * unit_rows, axis=-1, keepdims=True)
    )
    return (grad_in, jnp.sum(grad_out * unit_rows, axis=0), jnp.sum(grad_out, axis=0))


def block_shape(seq_total):
    block_count = max(1, seq_total // 512)
    return (block_count, seq_total // block_count)


def allowed_block(begin_at, block_len, seg_ids):
    q_pos = begin_at + jnp.arange(block_len)
    k_pos = jnp.arange(seg_ids.shape[0])
    q_seg = seg_ids[begin_at : begin_at + block_len]
    return (k_pos[None, :] <= q_pos[:, None]) & (q_seg[:, None] == seg_ids[None, :])


def attention_forward(queries, key_rows, value_rows, seg_ids):
    block_count, block_len = block_shape(queries.shape[0])
    pieces, totals = ([], [])
    for block_no in range(block_count):
        begin_at = block_no * block_len
        scores = jnp.einsum(
            "qhd,khd->hqk",
            queries[begin_at : begin_at + block_len],
            key_rows,
            preferred_element_type=jnp.float32,
        )
        scores = jnp.where(allowed_block(begin_at, block_len, seg_ids)[None], scores, -1e30)
        row_top = jnp.max(scores, axis=-1, keepdims=True)
        weights = jnp.exp(scores - row_top)
        summed = jnp.sum(weights, axis=-1, keepdims=True)
        prob_rows = (weights / summed).astype(jnp.bfloat16)
        pieces.append(
            jnp.einsum("hqk,khd->qhd", prob_rows, value_rows, preferred_element_type=jnp.float32)
        )
        totals.append(row_top + jnp.log(summed))
    return (jnp.concatenate(pieces, axis=0), jnp.concatenate(totals, axis=1))


def attention_backward(queries, key_rows, value_rows, seg_ids, totals, grad_mixed):
    block_count, block_len = block_shape(queries.shape[0])
    grad_queries = []
    grad_keys = jnp.zeros(key_rows.shape, jnp.float32)
    grad_values = jnp.zeros(value_rows.shape, jnp.float32)
    for block_no in range(block_count):
        begin_at = block_no * block_len
        part_query = queries[begin_at : begin_at + block_len]
        part_grad = grad_mixed[begin_at : begin_at + block_len]
        scores = jnp.einsum(
            "qhd,khd->hqk", part_query, key_rows, preferred_element_type=jnp.float32
        )
        scores = jnp.where(allowed_block(begin_at, block_len, seg_ids)[None], scores, -1e30)
        prob_exact = jnp.exp(scores - totals[:, begin_at : begin_at + block_len])
        prob_rows = prob_exact.astype(jnp.bfloat16)
        grad_probs = jnp.einsum(
            "qhd,khd->hqk", part_grad, value_rows, preferred_element_type=jnp.float32
        )
        row_dot = jnp.sum(prob_exact * grad_probs, axis=-1, keepdims=True)
        grad_scores = (prob_exact * (grad_probs - row_dot)).astype(jnp.bfloat16)
        grad_queries.append(
            jnp.einsum("hqk,khd->qhd", grad_scores, key_rows, preferred_element_type=jnp.float32)
        )
        grad_keys = grad_keys + jnp.einsum(
            "hqk,qhd->khd", grad_scores, part_query, preferred_element_type=jnp.float32
        )
        grad_values = grad_values + jnp.einsum(
            "hqk,qhd->khd", prob_rows, part_grad, preferred_element_type=jnp.float32
        )
    return (jnp.concatenate(grad_queries, axis=0), grad_keys, grad_values)


def layer_forward(rows_in, seg_ids, params):
    small, qkv_mat, out_mat, up_mat, down_mat = params
    gains, shifts, qv_rows, up_shift = small
    seq_total, model_width = rows_in.shape
    local_width = out_mat.shape[0]
    head_count = local_width // HEAD
    q_scale = HEAD ** (-0.5)
    rows_in = rows_in.astype(jnp.float32)
    normed, unit1, inv1 = norm_forward(rows_in, gains[0], shifts[0])
    normed = normed.astype(jnp.bfloat16)
    projected = jnp.dot(normed, qkv_mat, preferred_element_type=jnp.float32).reshape(
        seq_total, 3, local_width
    )
    queries = ((projected[:, 0] + qv_rows[0]) * q_scale).astype(jnp.bfloat16)
    key_rows = projected[:, 1].astype(jnp.bfloat16)
    value_rows = (projected[:, 2] + qv_rows[1]).astype(jnp.bfloat16)
    heads = (seq_total, head_count, HEAD)
    queries, key_rows, value_rows = (v.reshape(heads) for v in (queries, key_rows, value_rows))
    mixed, totals = attention_forward(queries, key_rows, value_rows, seg_ids)
    mixed = mixed.reshape(seq_total, local_width).astype(jnp.bfloat16)
    branch = pair_sum(jnp.dot(mixed, out_mat, preferred_element_type=jnp.float32))
    middle = rows_in + branch + shifts[2]
    normed2, unit2, inv2 = norm_forward(middle, gains[1], shifts[1])
    normed2 = normed2.astype(jnp.bfloat16)
    hidden = jnp.dot(normed2, up_mat, preferred_element_type=jnp.float32) + up_shift
    active = smooth(hidden).astype(jnp.bfloat16)
    branch2 = pair_sum(jnp.dot(active, down_mat, preferred_element_type=jnp.float32))
    output = (middle + branch2 + shifts[3]).astype(jnp.bfloat16)
    kept = (
        unit1, inv1, normed, queries, key_rows, value_rows, totals, mixed,
        unit2, inv2, normed2, hidden, active,
    )
    return (output, kept)


def layer_backward(grad_rows, seg_ids, params, kept):
    small, qkv_mat, out_mat, up_mat, down_mat = params
    gains = small[0]
    (
        unit1, inv1, normed, queries, key_rows, value_rows, totals, mixed,
        unit2, inv2, normed2, hidden, active,
    ) = kept
    seq_total = grad_rows.shape[0]
    local_width = out_mat.shape[0]
    heads = queries.shape
    q_scale = HEAD ** (-0.5)
    incoming = grad_rows.astype(jnp.float32)
    ignored, gelu_back = jax.vjp(smooth, hidden)
    grad_active = dot_last(grad_rows, down_mat)
    g_down = dot_rows(active, grad_rows)
    grad_hidden = gelu_back(grad_active)[0].astype(jnp.bfloat16)
    grad_normed2 = pair_sum(dot_last(grad_hidden, up_mat))
    g_up = dot_rows(normed2, grad_hidden)
    g_upb = jnp.sum(grad_hidden.astype(jnp.float32), axis=0)
    norm2_grad, gain2, shift2 = norm_backward(grad_normed2, unit2, inv2, gains[1])
    grad_middle = incoming + norm2_grad
    grad_branch = grad_middle.astype(jnp.bfloat16)
    grad_mixed = dot_last(grad_branch, out_mat).astype(jnp.bfloat16).reshape(heads)
    g_out = dot_rows(mixed, grad_branch)
    grad_queries, grad_keys, grad_values = attention_backward(
        queries, key_rows, value_rows, seg_ids, totals, grad_mixed
    )
    grad_queries = (grad_queries * q_scale).astype(jnp.bfloat16).reshape(seq_total, local_width)
    grad_keys = grad_keys.astype(jnp.bfloat16).reshape(seq_total, local_width)
    grad_values = grad_values.astype(jnp.bfloat16).reshape(seq_total, local_width)
    grad_proj = jnp.concatenate([grad_queries, grad_keys, grad_values], axis=1)
    grad_normed = pair_sum(dot_last(grad_proj, qkv_mat))
    g_qkv = dot_rows(normed, grad_proj)
    g_qv = jnp.stack(
        [
            jnp.sum(grad_queries.astype(jnp.float32), axis=0),
            jnp.sum(grad_values.astype(jnp.float32), axis=0),
        ]
    )
    norm1_grad, gain1, shift1 = norm_backward(grad_normed, unit1, inv1, gains[0])
    grad_in = (grad_middle + norm1_grad).astype(jnp.bfloat16)
    g_shift = jnp.stack(
        [
            shift1,
            shift2,
            jnp.sum(grad_branch.astype(jnp.float32), axis=0),
            jnp.sum(incoming, axis=0),
        ]
    )
    big = (g_qkv, g_out, g_up, g_down)
    return (grad_in, big, (g_qv, g_upb, jnp.stack([gain1, gain2]), g_shift))


def local(
    inputs,
    segments,
    cotangent,
    norm_gains,
    shared_biases,
    w_qkv,
    qv_bias,
    w_out,
    w_up,
    up_bias,
    w_down,
):
    s, x = lax.axis_index("section"), lax.axis_index("tensor")
    model_width = inputs.shape[2]
    local_width = w_qkv.shape[3]
    qkv_own = w_qkv[0].reshape(model_width, 3 * local_width)
    small_own = jnp.concatenate(
        [norm_gains[0].ravel(), shared_biases[0].ravel(), qv_bias[0].ravel(), up_bias[0].ravel()]
    )
    small_own = small_own.reshape(-1, model_width)
    rows = whole_rows(inputs)
    seg_ids = jnp.where(x == 0, segments[0], segments[1])

    def layer_params(layer):
        small = spread(layer, small_own).astype(jnp.float32)
        tail = small[6:].ravel()
        small = (
            small[:2],
            small[2:6],
            tail[: 2 * local_width].reshape(2, local_width),
            tail[2 * local_width :],
        )
        return (small,) + tuple(spread(layer, w) for w in (qkv_own, w_out[0], w_up[0], w_down[0]))

    params = [layer_params(layer) for layer in range(2)]
    outputs, kept_all = [], []
    for layer in range(2):
        rows, kept = layer_forward(rows, seg_ids, params[layer])
        outputs.append(rows)
        kept_all.append(kept)
    grad = whole_rows(cotangent)
    grads_in, bigs, smalls = [None, None], [None, None], [None, None]
    for layer in (1, 0):
        grad, big, smalls[layer] = layer_backward(grad, seg_ids, params[layer], kept_all[layer])
        grads_in[layer] = grad
        parts = tuple(collect(g) for g in big)
        if layer == 0:
            parts, bigs[1] = lax.optimization_barrier((parts, bigs[1]))
        bigs[layer] = lax.psum(parts, "dp")

    full = []
    for index in range(4):
        mine = jnp.where(s == 0, bigs[0][index], bigs[1][index])
        away = flip(jnp.where(s == 0, bigs[1][index], bigs[0][index]), "section")
        both = [jnp.where(s == 0, mine, away), jnp.where(s == 0, away, mine)]
        full.append(jnp.concatenate(both, axis=0).astype(jnp.float32))
    g_qkv, g_out, g_up, g_down = full

    packed = []
    for layer in range(2):
        g_qv, g_upb, g_gain, g_shift = smalls[layer]
        half = jnp.concatenate([g_qv.ravel(), g_upb]).reshape(-1, model_width)
        common = jnp.concatenate([g_gain, g_shift])
        packed.append(
            jnp.concatenate(
                [
                    jnp.where(s == 0, common, 0.0),
                    jnp.where(s == 0, half, 0.0),
                    jnp.where(s == 1, half, 0.0),
                ]
            )
        )
    packed = lax.psum(jnp.stack(packed), ("section", "tensor", "dp"))
    packed = jnp.where(s == 0, packed[0], packed[1])
    count = (packed.shape[0] - 6) // 2
    half = jnp.where(x == 0, packed[6 : 6 + count], packed[6 + count :]).ravel()
    return (
        placed_rows(outputs),
        placed_rows(grads_in),
        g_qkv.reshape(model_width, 3, local_width)[None],
        half[: 2 * local_width].reshape(2, local_width)[None],
        g_out[None],
        g_up[None],
        half[2 * local_width :][None],
        g_down[None],
        packed[:2][None],
        packed[2:6][None],
    )


def solution(mesh):
    return jax.shard_map(
        local,
        mesh=mesh,
        in_specs=(
            P("dp", "tensor", None),
            P("dp", None),
            P("dp", "tensor", None),
            P("section", None, None),
            P("section", None, None),
            P("section", None, None, "tensor"),
            P("section", None, "tensor"),
            P("section", "tensor", None),
            P("section", None, "tensor"),
            P("section", "tensor"),
            P("section", "tensor", None),
        ),
        out_specs=(
            P("section", "dp", "tensor", None),
            P("section", "dp", "tensor", None),
            P("section", None, None, "tensor"),
            P("section", None, "tensor"),
            P("section", "tensor", None),
            P("section", None, "tensor"),
            P("section", "tensor"),
            P("section", "tensor", None),
            P("section", None, None),
            P("section", None, None),
        ),
        check_vma=False,
    )
```

time: 1570 us -> 949 us (0.60)
  waiting for transfers between devices: 883 us -> 304 us
  starting transfers between devices: 8.31 us -> 210 us
  matrix products: 325 us -> 216 us
  blocking collectives: 100 us -> 0 us
  local copies, waits for them, and re-layouts: 62.7 us -> 40.4 us
  other arithmetic: 167 us -> 149 us
    all_gather x12 -> x0, waiting for transfers between devices: 283 us -> none  [the longest x3 79 us: local(): lax.all_gather(forward_normed2, 'tensor', axis=0, tiled=True)]
    reduce_scatter x12 -> x0, waiting for transfers between devices: 260 us -> none  [the longest x3 77.8 us: local(): lax.psum_scatter(jnp.dot(forward_mixed_rows, out_mat, preferred_element_t...]
    ppermute x4 -> x52, starting transfers between devices: 6.17 us -> 210 us  [the longest x10 66.6 us: spread(): lax.ppermute(block, GROUP, [(layer * 2 + t, t * 2 + t) for t in range(2)])]
    psum x2 -> x0, blocking collectives: 100 us -> none  [the longest x1 76.4 us: local(): g_gain, g_shift = lax.psum((g_gain, g_shift), ('tensor', 'dp'))]
    psum x1 -> x3, waiting for transfers between devices: 331 us -> 246 us  [the longest x2 139 us: local(): bigs[layer] = lax.psum(parts, 'dp')]
    ppermute x4 -> x52, waiting for transfers between devices: 9.45 us -> 58.5 us  [the longest x8 51 us: collect(): lax.ppermute(other, GROUP, [(c * 2 + x, (1 - x) * 2 + c) for c in range(2...]
    dot_general x12 -> x8, matrix products: 61.3 us -> 26.8 us  [dot_rows(): lax.dot_general(left, right, (((0,), (0,)), ((), ())), preferred_element_...]
    dot_general x6 -> x4, matrix products: 63 us -> 33.2 us  [attention_backward(): jnp.einsum('qhd,khd->hqk', part_grad, value_rows, preferred_element_type=...]
  transfers between devices with their start and end apart: 29 -> 55, of which waited for: 26 -> 6; matrix products, arithmetic and copies ran while one was open for 11% -> 40% of each run, Pallas kernels for 0% -> 0%
where the time goes in v1:
time: 949 us; the launch traced here: 936 us
  waiting for transfers between devices  304 us (32%)
  matrix products  216 us (23%)
  starting transfers between devices  210 us (22%)
  other arithmetic  149 us (16%)
  local copies, waits for them, and re-layouts  40.4 us (4%)
  between operations  16.3 us (2%)
    psum x2, waiting for transfers between devices, local(): bigs[layer] = lax.psum(parts, 'dp')  139 us
    psum x1, waiting for transfers between devices, local(): packed = lax.psum(jnp.stack(packed), ('section', 'tensor', 'dp'))  106 us
    ppermute x10, starting transfers between devices, spread(): lax.ppermute(block, GROUP, [(layer * 2 + t, t * 2 + t) for t in range(2)])  66.6 us
    ppermute x16, starting transfers between devices, flip(): return lax.ppermute(block, axis, [(0, 1), (1, 0)])  53 us
    ppermute x8, waiting for transfers between devices, collect(): lax.ppermute(other, GROUP, [(c * 2 + x, (1 - x) * 2 + c) for c in range(2...  51 us
    dot_general x8, matrix products, dot_last(): lax.dot_general(left, right, (((1,), (1,)), ((), ())), preferred_element_...  39.6 us
    ppermute x8, starting transfers between devices, collect(): lax.ppermute(same, GROUP, [(c * 2 + x, x * 2 + c) for c in range(2) for x...  37.6 us
    convert_element_type x3, other arithmetic, attention_backward(): grad_scores = (prob_exact * (grad_probs - row_dot)).astype(jnp.bfloat16)  37 us
  transfers between devices with their start and end apart: 55, of which 6 were waited for; matrix products, arithmetic and copies ran while one was open for 40% of the time, Pallas kernels for 0%

profile of v1, /device:TPU:0, one launch (start us, length us, event | category | flops | bytes accessed | tf_op | source)
XLA Modules:
  0.0 935.7 jit_solution(12917857345779766297)
XLA Ops:
  23.2 14.7 %collective-permute-start.3 = (bf16[768,1152]{0,1:T(8,128)(2,1)}, bf16[768,1152]{0,1:T(8,128)(2,1)}, u32[]{:S(2)}, u32[]{:S(2)}) collective-permute-start(bf16[768,1152]{0,1:T(8,128)(2,1)} %bitcast.2), channel_id=1, source_target_pairs={{0,0},{8,24},{1,1},{9,25},{2,2},{10,26},{3,3},{11,27},{4,4},{12,28... | collective-permute-start | bytes 5308424 | tf_op jit(solution)/shard_map/ppermute | solution.py:20
  46.1 5.9 collective-permute-start.5
  52.3 7.4 collective-permute-done
  96.4 19.1 %collective-permute-start.8 = (bf16[768,1536]{1,0:T(8,128)(2,1)}, bf16[768,1536]{1,0:T(8,128)(2,1)}, u32[]{:S(2)}, u32[]{:S(2)}) collective-permute-start(bf16[768,1536]{1,0:T(8,128)(2,1)} %bitcast.16), channel_id=1, source_target_pairs={{0,0},{8,24},{1,1},{9,25},{2,2},{10,26},{3,3},{11,27},{4,4},{12,28... | collective-permute-start | bytes 7077896 | tf_op jit(solution)/shard_map/ppermute | solution.py:20
  118.3 19.1 %collective-permute-start.10 = (bf16[1536,768]{1,0:T(8,128)(2,1)}, bf16[1536,768]{1,0:T(8,128)(2,1)}, u32[]{:S(2)}, u32[]{:S(2)}) collective-permute-start(bf16[1536,768]{1,0:T(8,128)(2,1)} %bitcast.17), channel_id=1, source_target_pairs={{0,0},{8,24},{1,1},{9,25},{2,2},{10,26},{3,3},{11,27},{4,4},{12,28... | collective-permute-start | bytes 7077896 | tf_op jit(solution)/shard_map/ppermute | solution.py:20
  147.5 8.5 convolution_convert_fusion.13
  205.1 23.2 %collective-permute-start.19 = (bf16[1024,768]{0,1:T(8,128)(2,1)}, bf16[1024,768]{0,1:T(8,128)(2,1)}, u32[]{:S(2)}, u32[]{:S(2)}) collective-permute-start(bf16[1024,768]{0,1:T(8,128)(2,1)} %convolution_convert_fusion.6), channel_id=1, source_target_pairs={{0,16},{16,0},{1,17},{17,1},{2,18},{18,2},{3,19},{19,3},{4,20},{20... | collective-permute-start | bytes 4718600 | tf_op jit(solution)/shard_map/ppermute | solution.py:16
  241.4 5.6 fusion.115
  252.4 18.5 %collective-permute-start.47 = (bf16[768,768]{1,0:T(8,128)(2,1)S(1)}, bf16[768,768]{1,0:T(8,128)(2,1)S(1)}, u32[]{:S(2)}, u32[]{:S(2)}) collective-permute-start(bf16[768,768]{1,0:T(8,128)(2,1)S(1)} %get-tuple-element.109), channel_id=1, source_target_pairs={{0,16},{8,0},{16,24},{24,8},{1,17},{9,1},{17,25},{25,9},{2,18},{10... | collective-permute-start | bytes 3538952 | tf_op jit(solution)/shard_map/ppermute | solution.py:38
  270.9 7.4 convert_reduce_fusion
  285.7 24.3 %collective-permute-start.27 = (bf16[1024,768]{0,1:T(8,128)(2,1)S(1)}, bf16[1024,768]{0,1:T(8,128)(2,1)S(1)}, u32[]{:S(2)}, u32[]{:S(2)}) collective-permute-start(bf16[1024,768]{0,1:T(8,128)(2,1)S(1)} %convolution_convert_fusion.11), channel_id=1, source_target_pairs={{0,16},{16,0},{1,17},{17,1},{2,18},{18,2},{3,19},{19,3},{4,20},{20... | collective-permute-start | bytes 4718600 | tf_op jit(solution)/shard_map/ppermute | solution.py:16
  312.6 7.3 convolution_convert_fusion.12
  321.9 18.6 %collective-permute-done.45 = bf16[384,1536]{1,0:T(8,128)(2,1)S(1)} collective-permute-done((bf16[384,1536]{1,0:T(8,128)(2,1)S(1)}, bf16[384,1536]{1,0:T(8,128)(2,1)S(1)}, u32[]{:S(2)}, u32[]{:S(2)}) %collective-permute-start.45) | collective-permute-done | bytes 1179680 | tf_op jit(solution)/shard_map/ppermute | solution.py:38
  351.4 6.8 multiply_reduce_fusion.3
  358.1 10.4 %multiply_convert_fusion.3 = bf16[6,512,1024]{2,1,0:T(8,128)(2,1)} fusion(f32[6,512,1024]{2,1,0:T(8,128)} %get-tuple-element.164, f32[6,512,1024]{2,1,0:T(8,128)S(1)} %bitcast.167, f32[6,512]{1,0:T(8,128)S(1)} %get-tuple-element.163, f32[6,512]{1,0:T(8,128)S(1)} %log_add_fusion.3, pred[512,1024]{1,0:T(8,128)(4,1)S(1)} %copy-done.9), kind=kLoop, calls=%fused_computation.9 | loop fusion | flops 15728640 | bytes 32006144 | tf_op jit(solution)/shard_map/convert_element_type | solution.py:149
  368.5 5.9 fusion.158
  383.8 8.2 multiply_reduce_fusion.2
  395.5 5.4 convert_reduce_fusion.8
  401.0 9.6 %multiply_convert_fusion.2 = bf16[6,512,1024]{2,1,0:T(8,128)(2,1)S(1)} fusion(f32[6,512,1024]{2,1,0:T(8,128)} %get-tuple-element.166, f32[6,512,1024]{2,1,0:T(8,128)} %copy-done.1, f32[6,512]{1,0:T(8,128)S(1)} %get-tuple-element.165, f32[6,512]{1,0:T(8,128)S(1)} %log_add_fusion.2, pred[512,1024]{1,0:T(8,128)(4,1)S(1)} %copy-done.12), kind=kLoop, calls=%fused_computation.6 | loop fusion | flops 15728640 | bytes 32006144 | tf_op jit(solution)/shard_map/convert_element_type | solution.py:149
  450.7 10.5 %collective-permute-start.38 = (bf16[768,768]{1,0:T(8,128)(2,1)}, bf16[768,768]{1,0:T(8,128)(2,1)}, u32[]{:S(2)}, u32[]{:S(2)}) collective-permute-start(bf16[768,768]{1,0:T(8,128)(2,1)} %get-tuple-element.112), channel_id=1, source_target_pairs={{0,0},{8,16},{16,8},{24,24},{1,1},{9,17},{17,9},{25,25},{2,2},{10,... | collective-permute-start | bytes 3538952 | tf_op jit(solution)/shard_map/ppermute | solution.py:37
  461.3 8.6 convert_reduce_fusion.1
  473.1 5.5 convolution_convert_fusion.9
  480.2 10.3 %collective-permute-start.36 = (bf16[384,1536]{1,0:T(8,128)(2,1)}, bf16[384,1536]{1,0:T(8,128)(2,1)}, u32[]{:S(2)}, u32[]{:S(2)}) collective-permute-start(bf16[384,1536]{1,0:T(8,128)(2,1)} %get-tuple-element.114), channel_id=1, source_target_pairs={{0,0},{8,16},{16,8},{24,24},{1,1},{9,17},{17,9},{25,25},{2,2},{10,... | collective-permute-start | bytes 3538952 | tf_op jit(solution)/shard_map/ppermute | solution.py:37
  498.0 21.7 %collective-permute-done.37 = bf16[384,1536]{1,0:T(8,128)(2,1)} collective-permute-done((bf16[384,1536]{1,0:T(8,128)(2,1)}, bf16[384,1536]{1,0:T(8,128)(2,1)}, u32[]{:S(2)}, u32[]{:S(2)}) %collective-permute-start.37) | collective-permute-done | bytes 1179680 | tf_op jit(solution)/shard_map/ppermute | solution.py:38
  534.4 7.9 fusion.8
  542.3 10.4 %multiply_reduce_fusion = (f32[6,512]{1,0:T(8,128)}, f32[6,512,1024]{2,1,0:T(8,128)}) fusion(f32[6,512,1024]{2,1,0:T(8,128)} %copy-done.3, f32[6,512]{1,0:T(8,128)S(1)} %copy-done.76, pred[512,1024]{1,0:T(8,128)(4,1)S(1)} %copy-done.13, bf16[512,6,64]{0,2,1:T(8,128)(2,1)S(1)} %bitcast.199, bf16[1024,6,64]{0,2,1:T(8,128)(2,1)S(1)} %copy-done.35), kind=kOutput, calls=%fused_computation.1 | convolution fusion | flops 415233024 | bytes 26894336 | tf_op jit(solution)/shard_map/qhd,khd->hqk/dot_general | solution.py:145
  552.7 7.9 multiply_reduce_fusion.1
  560.6 17.0 %multiply_convert_fusion = (bf16[6,512,1024]{2,1,0:T(8,128)(2,1)}, bf16[6,512,1024]{2,1,0:T(8,128)(2,1)S(1)}) fusion(f32[6,512,1024]{2,1,0:T(8,128)} %get-tuple-element.170, f32[6,512,1024]{2,1,0:T(8,128)} %copy-done.3, f32[6,512]{1,0:T(8,128)} %get-tuple-element.169, f32[6,512]{1,0:T(8,128)} %log_add_fusion, pred[512,1024]{1,0:T(8,128)(4,1)} %copy-done.11, ...), kind=kLoop, calls=%fused_computation | loop fusion | flops 31457280 | bytes 64012288 | tf_op jit(solution)/shard_map/convert_element_type | solution.py:149
  616.5 8.4 collective-permute-start.32
  630.7 10.6 %collective-permute-done.33 = bf16[384,1152]{1,0:T(8,128)(2,1)} collective-permute-done((bf16[384,1152]{1,0:T(8,128)(2,1)}, bf16[384,1152]{1,0:T(8,128)(2,1)}, u32[]{:S(2)}, u32[]{:S(2)}) %collective-permute-start.33) | collective-permute-done | bytes 884768 | tf_op jit(solution)/shard_map/ppermute | solution.py:38
  654.2 106.2 %all-reduce.6.cloned.1.call-done = f32[2,12,768]{2,1,0:T(8,128)} async-done(((f32[2,12,768]{2,1,0:T(8,128)}), f32[2,12,768]{2,1,0:T(8,128)}) %all-reduce.6.cloned.1.call-update) | async-done | bytes 73744 | tf_op jit(solution)/shard_map/psum | solution.py:323
  766.9 139.3 %all-reduce.8.cloned.1.call-done = (bf16[384,1152]{1,0:T(8,128)(2,1)}, bf16[192,768]{1,0:T(8,128)(2,1)}, bf16[384,1536]{1,0:T(8,128)(2,1)}, bf16[768,768]{1,0:T(8,128)(2,1)}) async-done(((bf16[384,1152]{1,0:T(8,128)(2,1)}, bf16[192,768]{1,0:T(8,128)(2,1)}, bf16[384,1536]{1,0:T(8,128)(2,1)}, bf16[768,768]{1,0:T(8,128)(2,1)}), (bf16[384,1152]{1,0:T(8,128)(2,1)}, bf16[192,768]{1,0:T(8,128)(2,1)}, ...) | async-done | bytes 3538960 | tf_op jit(solution)/shard_map/psum | solution.py:299
  (556 shorter events, 329.2 us)
Async XLA Ops:
  7.2 636.7 %all-reduce.10.cloned.1.call-start = ((), (), s32[]{:S(2)}) async-start(), calls=%async_computation.2 | async-start | bytes 7077888 | tf_op jit(solution)/shard_map/psum | solution.py:299
  10.1 31.3 %collective-permute-start.2 = (bf16[9,768]{1,0:T(8,128)(2,1)S(1)}, bf16[9,768]{1,0:T(8,128)(2,1)S(1)}, u32[]{:S(2)}, u32[]{:S(2)}) collective-permute-start(bf16[9,768]{1,0:T(8,128)(2,1)S(1)} %reshape.489), channel_id=1, source_target_pairs={{0,8},{8,16},{1,9},{9,17},{2,10},{10,18},{3,11},{11,19},{4,12},{12... | collective-permute-start | bytes 41480 | tf_op jit(solution)/shard_map/ppermute | solution.py:21
  19.5 42.3 %collective-permute-start.4 = (bf16[768,1152]{0,1:T(8,128)(2,1)}, bf16[768,1152]{0,1:T(8,128)(2,1)}, u32[]{:S(2)}, u32[]{:S(2)}) collective-permute-start(bf16[768,1152]{0,1:T(8,128)(2,1)} %bitcast.2), channel_id=1, source_target_pairs={{0,8},{8,16},{1,9},{9,17},{2,10},{10,18},{3,11},{11,19},{4,12},{12... | collective-permute-start | bytes 5308424 | tf_op jit(solution)/shard_map/ppermute | solution.py:21
  23.2 38.5 %collective-permute-start.3 = (bf16[768,1152]{0,1:T(8,128)(2,1)}, bf16[768,1152]{0,1:T(8,128)(2,1)}, u32[]{:S(2)}, u32[]{:S(2)}) collective-permute-start(bf16[768,1152]{0,1:T(8,128)(2,1)} %bitcast.2), channel_id=1, source_target_pairs={{0,0},{8,24},{1,1},{9,25},{2,2},{10,26},{3,3},{11,27},{4,4},{12,28... | collective-permute-start | bytes 5308424 | tf_op jit(solution)/shard_map/ppermute | solution.py:20
  41.4 46.6 %collective-permute-start.6 = (bf16[384,768]{1,0:T(8,128)(2,1)}, bf16[384,768]{1,0:T(8,128)(2,1)}, u32[]{:S(2)}, u32[]{:S(2)}) collective-permute-start(bf16[384,768]{1,0:T(8,128)(2,1)} %bitcast.226), channel_id=1, source_target_pairs={{0,8},{8,16},{1,9},{9,17},{2,10},{10,18},{3,11},{11,19},{4,12},{12... | collective-permute-start | bytes 1769480 | tf_op jit(solution)/shard_map/ppermute | solution.py:21
  46.1 41.9 %collective-permute-start.5 = (bf16[384,768]{1,0:T(8,128)(2,1)}, bf16[384,768]{1,0:T(8,128)(2,1)}, u32[]{:S(2)}, u32[]{:S(2)}) collective-permute-start(bf16[384,768]{1,0:T(8,128)(2,1)} %bitcast.227), channel_id=1, source_target_pairs={{0,0},{8,24},{1,1},{9,25},{2,2},{10,26},{3,3},{11,27},{4,4},{12,28... | collective-permute-start | bytes 1769480 | tf_op jit(solution)/shard_map/ppermute | solution.py:20
  91.0 46.4 %collective-permute-start.7 = (bf16[1024,768]{0,1:T(8,128)(2,1)S(1)}, bf16[1024,768]{0,1:T(8,128)(2,1)S(1)}, u32[]{:S(2)}, u32[]{:S(2)}) collective-permute-start(bf16[1024,768]{0,1:T(8,128)(2,1)S(1)} %convolution_convert_fusion.7), channel_id=1, source_target_pairs={{0,16},{16,0},{1,17},{17,1},{2,18},{18,2},{3,19},{19,3},{4,20},{20... | collective-permute-start | bytes 4718600 | tf_op jit(solution)/shard_map/ppermute | solution.py:16
  91.1 51.0 %collective-permute-start.9 = (bf16[768,1536]{1,0:T(8,128)(2,1)}, bf16[768,1536]{1,0:T(8,128)(2,1)}, u32[]{:S(2)}, u32[]{:S(2)}) collective-permute-start(bf16[768,1536]{1,0:T(8,128)(2,1)} %bitcast.16), channel_id=1, source_target_pairs={{0,8},{8,16},{1,9},{9,17},{2,10},{10,18},{3,11},{11,19},{4,12},{12... | collective-permute-start | bytes 7077896 | tf_op jit(solution)/shard_map/ppermute | solution.py:21
  96.4 45.7 %collective-permute-start.8 = (bf16[768,1536]{1,0:T(8,128)(2,1)}, bf16[768,1536]{1,0:T(8,128)(2,1)}, u32[]{:S(2)}, u32[]{:S(2)}) collective-permute-start(bf16[768,1536]{1,0:T(8,128)(2,1)} %bitcast.16), channel_id=1, source_target_pairs={{0,0},{8,24},{1,1},{9,25},{2,2},{10,26},{3,3},{11,27},{4,4},{12,28... | collective-permute-start | bytes 7077896 | tf_op jit(solution)/shard_map/ppermute | solution.py:20
  115.5 32.0 %collective-permute-start.11 = (bf16[1536,768]{1,0:T(8,128)(2,1)}, bf16[1536,768]{1,0:T(8,128)(2,1)}, u32[]{:S(2)}, u32[]{:S(2)}) collective-permute-start(bf16[1536,768]{1,0:T(8,128)(2,1)} %bitcast.17), channel_id=1, source_target_pairs={{0,8},{8,16},{1,9},{9,17},{2,10},{10,18},{3,11},{11,19},{4,12},{12... | collective-permute-start | bytes 7077896 | tf_op jit(solution)/shard_map/ppermute | solution.py:21
  169.1 31.8 %collective-permute-start.18 = (bf16[384,768]{1,0:T(8,128)(2,1)}, bf16[384,768]{1,0:T(8,128)(2,1)}, u32[]{:S(2)}, u32[]{:S(2)}) collective-permute-start(bf16[384,768]{1,0:T(8,128)(2,1)} %bitcast.228), channel_id=1, source_target_pairs={{16,8},{24,16},{17,9},{25,17},{18,10},{26,18},{19,11},{27,19},{20,... | collective-permute-start | bytes 1769480 | tf_op jit(solution)/shard_map/ppermute | solution.py:21
  173.2 60.6 %collective-permute-start.26 = (bf16[512,768]{0,1:T(8,128)(2,1)}, bf16[512,768]{0,1:T(8,128)(2,1)}, u32[]{:S(2)}, u32[]{:S(2)}) collective-permute-start(bf16[512,768]{0,1:T(8,128)(2,1)} %select_bitcast_fusion.6), channel_id=1, source_target_pairs={{0,8},{8,0},{1,9},{9,1},{2,10},{10,2},{3,11},{11,3},{4,12},{12,4},... | collective-permute-start | bytes 2359304 | tf_op jit(solution)/shard_map/ppermute | solution.py:16
  205.1 32.8 %collective-permute-start.19 = (bf16[1024,768]{0,1:T(8,128)(2,1)}, bf16[1024,768]{0,1:T(8,128)(2,1)}, u32[]{:S(2)}, u32[]{:S(2)}) collective-permute-start(bf16[1024,768]{0,1:T(8,128)(2,1)} %convolution_convert_fusion.6), channel_id=1, source_target_pairs={{0,16},{16,0},{1,17},{17,1},{2,18},{18,2},{3,19},{19,3},{4,20},{20... | collective-permute-start | bytes 4718600 | tf_op jit(solution)/shard_map/ppermute | solution.py:16
  231.7 39.2 %collective-permute-start.23 = (bf16[1536,768]{1,0:T(8,128)(2,1)}, bf16[1536,768]{1,0:T(8,128)(2,1)}, u32[]{:S(2)}, u32[]{:S(2)}) collective-permute-start(bf16[1536,768]{1,0:T(8,128)(2,1)} %bitcast.17), channel_id=1, source_target_pairs={{16,8},{24,16},{17,9},{25,17},{18,10},{26,18},{19,11},{27,19},{20,... | collective-permute-start | bytes 7077896 | tf_op jit(solution)/shard_map/ppermute | solution.py:21
  233.8 37.1 %collective-permute-start.22 = (bf16[1536,768]{1,0:T(8,128)(2,1)}, bf16[1536,768]{1,0:T(8,128)(2,1)S(1)}, u32[]{:S(2)}, u32[]{:S(2)}) collective-permute-start(bf16[1536,768]{1,0:T(8,128)(2,1)} %bitcast.17), channel_id=1, source_target_pairs={{16,0},{24,24},{17,1},{25,25},{18,2},{26,26},{19,3},{27,27},{20,4}... | collective-permute-start | bytes 7077896 | tf_op jit(solution)/shard_map/ppermute | solution.py:20
  251.7 68.2 %collective-permute-start.46 = (bf16[768,768]{1,0:T(8,128)(2,1)S(1)}, bf16[768,768]{1,0:T(8,128)(2,1)S(1)}, u32[]{:S(2)}, u32[]{:S(2)}) collective-permute-start(bf16[768,768]{1,0:T(8,128)(2,1)S(1)} %get-tuple-element.108), channel_id=1, source_target_pairs={{0,0},{8,16},{16,8},{24,24},{1,1},{9,17},{17,9},{25,25},{2,2},{10,... | collective-permute-start | bytes 3538952 | tf_op jit(solution)/shard_map/ppermute | solution.py:37
  252.4 68.2 %collective-permute-start.47 = (bf16[768,768]{1,0:T(8,128)(2,1)S(1)}, bf16[768,768]{1,0:T(8,128)(2,1)S(1)}, u32[]{:S(2)}, u32[]{:S(2)}) collective-permute-start(bf16[768,768]{1,0:T(8,128)(2,1)S(1)} %get-tuple-element.109), channel_id=1, source_target_pairs={{0,16},{8,0},{16,24},{24,8},{1,17},{9,1},{17,25},{25,9},{2,18},{10... | collective-permute-start | bytes 3538952 | tf_op jit(solution)/shard_map/ppermute | solution.py:38
  285.7 56.1 %collective-permute-start.27 = (bf16[1024,768]{0,1:T(8,128)(2,1)S(1)}, bf16[1024,768]{0,1:T(8,128)(2,1)S(1)}, u32[]{:S(2)}, u32[]{:S(2)}) collective-permute-start(bf16[1024,768]{0,1:T(8,128)(2,1)S(1)} %convolution_convert_fusion.11), channel_id=1, source_target_pairs={{0,16},{16,0},{1,17},{17,1},{2,18},{18,2},{3,19},{19,3},{4,20},{20... | collective-permute-start | bytes 4718600 | tf_op jit(solution)/shard_map/ppermute | solution.py:16
  319.9 106.2 %collective-permute-start.24 = (bf16[1024,768]{0,1:T(8,128)(2,1)}, bf16[1024,768]{0,1:T(8,128)(2,1)}, u32[]{:S(2)}, u32[]{:S(2)}) collective-permute-start(bf16[1024,768]{0,1:T(8,128)(2,1)} %convolution_convert_fusion.12), channel_id=1, source_target_pairs={{0,16},{16,0},{1,17},{17,1},{2,18},{18,2},{3,19},{19,3},{4,20},{20... | collective-permute-start | bytes 4718600 | tf_op jit(solution)/shard_map/ppermute | solution.py:16
  393.9 40.8 %collective-permute-start.42 = (bf16[192,768]{1,0:T(8,128)(2,1)}, bf16[192,768]{1,0:T(8,128)(2,1)S(1)}, u32[]{:S(2)}, u32[]{:S(2)}) collective-permute-start(bf16[192,768]{1,0:T(8,128)(2,1)} %get-tuple-element.143), channel_id=1, source_target_pairs={{0,0},{8,16},{16,8},{24,24},{1,1},{9,17},{17,9},{25,25},{2,2},{10,... | collective-permute-start | bytes 884744 | tf_op jit(solution)/shard_map/ppermute | solution.py:37
  395.5 39.2 %collective-permute-start.43 = (bf16[192,768]{1,0:T(8,128)(2,1)}, bf16[192,768]{1,0:T(8,128)(2,1)}, u32[]{:S(2)}, u32[]{:S(2)}) collective-permute-start(bf16[192,768]{1,0:T(8,128)(2,1)} %get-tuple-element.144), channel_id=1, source_target_pairs={{0,16},{8,0},{16,24},{24,8},{1,17},{9,1},{17,25},{25,9},{2,18},{10... | collective-permute-start | bytes 884744 | tf_op jit(solution)/shard_map/ppermute | solution.py:38
  425.0 55.2 %collective-permute-start.40 = (bf16[384,1152]{1,0:T(8,128)(2,1)S(1)}, bf16[384,1152]{1,0:T(8,128)(2,1)S(1)}, u32[]{:S(2)}, u32[]{:S(2)}) collective-permute-start(bf16[384,1152]{1,0:T(8,128)(2,1)S(1)} %get-tuple-element.124), channel_id=1, source_target_pairs={{0,0},{8,16},{16,8},{24,24},{1,1},{9,17},{17,9},{25,25},{2,2},{10,... | collective-permute-start | bytes 2654216 | tf_op jit(solution)/shard_map/ppermute | solution.py:37
  426.1 64.4 %collective-permute-start.41 = (bf16[384,1152]{1,0:T(8,128)(2,1)S(1)}, bf16[384,1152]{1,0:T(8,128)(2,1)S(1)}, u32[]{:S(2)}, u32[]{:S(2)}) collective-permute-start(bf16[384,1152]{1,0:T(8,128)(2,1)S(1)} %get-tuple-element.125), channel_id=1, source_target_pairs={{0,16},{8,0},{16,24},{24,8},{1,17},{9,1},{17,25},{25,9},{2,18},{10... | collective-permute-start | bytes 2654216 | tf_op jit(solution)/shard_map/ppermute | solution.py:38
  450.7 42.4 %collective-permute-start.38 = (bf16[768,768]{1,0:T(8,128)(2,1)}, bf16[768,768]{1,0:T(8,128)(2,1)}, u32[]{:S(2)}, u32[]{:S(2)}) collective-permute-start(bf16[768,768]{1,0:T(8,128)(2,1)} %get-tuple-element.112), channel_id=1, source_target_pairs={{0,0},{8,16},{16,8},{24,24},{1,1},{9,17},{17,9},{25,25},{2,2},{10,... | collective-permute-start | bytes 3538952 | tf_op jit(solution)/shard_map/ppermute | solution.py:37
  461.2 33.9 %collective-permute-start.39 = (bf16[768,768]{1,0:T(8,128)(2,1)}, bf16[768,768]{1,0:T(8,128)(2,1)}, u32[]{:S(2)}, u32[]{:S(2)}) collective-permute-start(bf16[768,768]{1,0:T(8,128)(2,1)} %get-tuple-element.113), channel_id=1, source_target_pairs={{0,16},{8,0},{16,24},{24,8},{1,17},{9,1},{17,25},{25,9},{2,18},{10... | collective-permute-start | bytes 3538952 | tf_op jit(solution)/shard_map/ppermute | solution.py:38
  478.6 44.1 %collective-permute-start.29 = (bf16[1024,768]{0,1:T(8,128)(2,1)}, bf16[1024,768]{0,1:T(8,128)(2,1)}, u32[]{:S(2)}, u32[]{:S(2)}) collective-permute-start(bf16[1024,768]{0,1:T(8,128)(2,1)} %convolution_convert_fusion.9), channel_id=1, source_target_pairs={{0,16},{16,0},{1,17},{17,1},{2,18},{18,2},{3,19},{19,3},{4,20},{20... | collective-permute-start | bytes 4718600 | tf_op jit(solution)/shard_map/ppermute | solution.py:16
  491.7 268.7 %all-reduce.6.cloned.1.call-start = ((), (), s32[]{:S(2)}) async-start(), calls=%async_computation | async-start | bytes 196608 | tf_op jit(solution)/shard_map/psum | solution.py:323
  493.1 150.9 %collective-permute-start.25 = (bf16[512,768]{0,1:T(8,128)(2,1)}, bf16[512,768]{0,1:T(8,128)(2,1)}, u32[]{:S(2)}, u32[]{:S(2)}) collective-permute-start(bf16[512,768]{0,1:T(8,128)(2,1)} %broadcast_select_fusion.42), channel_id=1, source_target_pairs={{0,8},{8,0},{1,9},{9,1},{2,10},{10,2},{3,11},{11,3},{4,12},{12,4},... | collective-permute-start | bytes 2359304 | tf_op jit(solution)/shard_map/ppermute | solution.py:16
  586.2 38.6 %collective-permute-start.34 = (bf16[192,768]{1,0:T(8,128)(2,1)}, bf16[192,768]{1,0:T(8,128)(2,1)}, u32[]{:S(2)}, u32[]{:S(2)}) collective-permute-start(bf16[192,768]{1,0:T(8,128)(2,1)} %get-tuple-element.145), channel_id=1, source_target_pairs={{0,0},{8,16},{16,8},{24,24},{1,1},{9,17},{17,9},{25,25},{2,2},{10,... | collective-permute-start | bytes 884744 | tf_op jit(solution)/shard_map/ppermute | solution.py:37
  589.9 34.9 %collective-permute-start.35 = (bf16[192,768]{1,0:T(8,128)(2,1)}, bf16[192,768]{1,0:T(8,128)(2,1)}, u32[]{:S(2)}, u32[]{:S(2)}) collective-permute-start(bf16[192,768]{1,0:T(8,128)(2,1)} %get-tuple-element.146), channel_id=1, source_target_pairs={{0,16},{8,0},{16,24},{24,8},{1,17},{9,1},{17,25},{25,9},{2,18},{10... | collective-permute-start | bytes 884744 | tf_op jit(solution)/shard_map/ppermute | solution.py:38
  630.6 275.6 %all-reduce.8.cloned.1.call-start = ((), (), s32[]{:S(2)}) async-start(), calls=%async_computation.1 | async-start | bytes 7077888 | tf_op jit(solution)/shard_map/psum | solution.py:299
  654.1 109.5 %collective-permute-start.31 = (bf16[512,768]{0,1:T(8,128)(2,1)S(1)}, bf16[512,768]{0,1:T(8,128)(2,1)S(1)}, u32[]{:S(2)}, u32[]{:S(2)}) collective-permute-start(bf16[512,768]{0,1:T(8,128)(2,1)S(1)} %broadcast_select_fusion.40), channel_id=1, source_target_pairs={{0,8},{8,0},{1,9},{9,1},{2,10},{10,2},{3,11},{11,3},{4,12},{12,4},... | collective-permute-start | bytes 2359304 | tf_op jit(solution)/shard_map/ppermute | solution.py:16
  (148 other events, 2038.2 us)
Sparse Core Ops, SparseCore 0:
  491.9 142.4 all-reduce.9
  640.9 119.4 all-reduce.5
  764.9 141.3 all-reduce.7

commit v2 on v1

--- a/solution.py
+++ b/solution.py
@@ -296,7 +296,19 @@
         parts = tuple(collect(g) for g in big)
         if layer == 0:
             parts, bigs[1] = lax.optimization_barrier((parts, bigs[1]))
-        bigs[layer] = lax.psum(parts, "dp")
+            packed = jnp.stack(
+                [
+                    jnp.concatenate(
+                        [g_gain, g_shift, jnp.concatenate([g_qv.ravel(), g_upb]).reshape(-1, model_width)]
+                    )
+                    for g_qv, g_upb, g_gain, g_shift in smalls
+                ]
+            )
+            packed = (packed + flip(packed, "tensor")).astype(jnp.bfloat16)
+            *parts, packed = lax.psum((*parts, packed), "dp")
+            bigs[0] = tuple(parts)
+        else:
+            bigs[1] = lax.psum(parts, "dp")
 
     full = []
     for index in range(4):
@@ -306,24 +318,10 @@
         full.append(jnp.concatenate(both, axis=0).astype(jnp.float32))
     g_qkv, g_out, g_up, g_down = full
 
-    packed = []
-    for layer in range(2):
-        g_qv, g_upb, g_gain, g_shift = smalls[layer]
-        half = jnp.concatenate([g_qv.ravel(), g_upb]).reshape(-1, model_width)
-        common = jnp.concatenate([g_gain, g_shift])
-        packed.append(
-            jnp.concatenate(
-                [
-                    jnp.where(s == 0, common, 0.0),
-                    jnp.where(s == 0, half, 0.0),
-                    jnp.where(s == 1, half, 0.0),
-                ]
-            )
-        )
-    packed = lax.psum(jnp.stack(packed), ("section", "tensor", "dp"))
-    packed = jnp.where(s == 0, packed[0], packed[1])
-    count = (packed.shape[0] - 6) // 2
-    half = jnp.where(x == 0, packed[6 : 6 + count], packed[6 + count :]).ravel()
+    away = flip(packed, "section")
+    common = jnp.where(s == 0, packed[0, :6], packed[1, :6]).astype(jnp.float32)
+    half = jnp.where(s == x, packed, away)
+    half = jnp.where(s == 0, half[0, 6:], half[1, 6:]).astype(jnp.float32).ravel()
     return (
         placed_rows(outputs),
         placed_rows(grads_in),
@@ -333,8 +331,8 @@
         g_up[None],
         half[2 * local_width :][None],
         g_down[None],
-        packed[:2][None],
-        packed[2:6][None],
+        common[:2][None],
+        common[2:6][None],
     )
 
 

time: 949 us -> 801 us (0.84)
  waiting for transfers between devices: 304 us -> 133 us
  blocking collectives: 0 us -> 40.8 us
  matrix products: 216 us -> 200 us
    psum x3 -> x2, waiting for transfers between devices: 246 us -> 85 us  [the longest x1 85 us: local(): *parts, packed = lax.psum((*parts, packed), 'dp')]
    psum x0 -> x1, blocking collectives: none -> 40.8 us  [local(): *parts, packed = lax.psum((*parts, packed), 'dp')]
    ppermute x8, waiting for transfers between devices: 51 us -> 41 us  [collect(): lax.ppermute(other, GROUP, [(c * 2 + x, (1 - x) * 2 + c) for c in range(2...]
    unnamed x260 -> x244, local copies, waits for them, and re-layouts: 26.7 us -> 23.5 us
    ppermute x16 -> x18, starting transfers between devices: 53 us -> 55.4 us  [flip(): return lax.ppermute(block, axis, [(0, 1), (1, 0)])]
  transfers between devices with their start and end apart: 55 -> 56, of which waited for: 6 -> 6; matrix products, arithmetic and copies ran while one was open for 40% -> 45% of each run, Pallas kernels for 0% -> 0%
where the time goes in v2:
time: 801 us; the launch traced here: 787 us
  starting transfers between devices  217 us (27%)
  matrix products  200 us (25%)
  other arithmetic  141 us (18%)
  waiting for transfers between devices  133 us (17%)
  blocking collectives  40.8 us (5%)
  local copies, waits for them, and re-layouts  38.3 us (5%)
  between operations  16.9 us (2%)
    psum x1, waiting for transfers between devices, local(): *parts, packed = lax.psum((*parts, packed), 'dp')  85 us
    ppermute x10, starting transfers between devices, spread(): lax.ppermute(block, GROUP, [(layer * 2 + t, t * 2 + t) for t in range(2)])  66.8 us
    ppermute x18, starting transfers between devices, flip(): return lax.ppermute(block, axis, [(0, 1), (1, 0)])  55.4 us
    dot_general x8, matrix products, dot_last(): lax.dot_general(left, right, (((1,), (1,)), ((), ())), preferred_element_...  42.9 us
    ppermute x8, starting transfers between devices, collect(): lax.ppermute(same, GROUP, [(c * 2 + x, x * 2 + c) for c in range(2) for x...  42.3 us
    ppermute x8, waiting for transfers between devices, collect(): lax.ppermute(other, GROUP, [(c * 2 + x, (1 - x) * 2 + c) for c in range(2...  41 us
    psum x1, blocking collectives, local(): *parts, packed = lax.psum((*parts, packed), 'dp')  40.8 us
    dot_general x4, matrix products, attention_backward(): jnp.einsum('qhd,khd->hqk', part_grad, value_rows, preferred_element_type=...  33.1 us
  transfers between devices with their start and end apart: 56, of which 6 were waited for; matrix products, arithmetic and copies ran while one was open for 45% of the time, Pallas kernels for 0%

profile of v2, /device:TPU:0, one launch (start us, length us, event | category | flops | bytes accessed | tf_op | source)
XLA Modules:
  0.0 787.5 jit_solution(13224804184631433766)
XLA Ops:
  23.3 14.8 %collective-permute-start.3 = (bf16[768,1152]{0,1:T(8,128)(2,1)}, bf16[768,1152]{0,1:T(8,128)(2,1)}, u32[]{:S(2)}, u32[]{:S(2)}) collective-permute-start(bf16[768,1152]{0,1:T(8,128)(2,1)} %bitcast.2), channel_id=1, source_target_pairs={{0,0},{8,24},{1,1},{9,25},{2,2},{10,26},{3,3},{11,27},{4,4},{12,28... | collective-permute-start | bytes 5308424 | tf_op jit(solution)/shard_map/ppermute | solution.py:20
  46.3 6.0 collective-permute-start.5
  52.4 7.2 collective-permute-done
  96.3 19.3 %collective-permute-start.8 = (bf16[768,1536]{1,0:T(8,128)(2,1)}, bf16[768,1536]{1,0:T(8,128)(2,1)}, u32[]{:S(2)}, u32[]{:S(2)}) collective-permute-start(bf16[768,1536]{1,0:T(8,128)(2,1)} %bitcast.16), channel_id=1, source_target_pairs={{0,0},{8,24},{1,1},{9,25},{2,2},{10,26},{3,3},{11,27},{4,4},{12,28... | collective-permute-start | bytes 7077896 | tf_op jit(solution)/shard_map/ppermute | solution.py:20
  118.3 19.2 %collective-permute-start.10 = (bf16[1536,768]{1,0:T(8,128)(2,1)}, bf16[1536,768]{1,0:T(8,128)(2,1)}, u32[]{:S(2)}, u32[]{:S(2)}) collective-permute-start(bf16[1536,768]{1,0:T(8,128)(2,1)} %bitcast.17), channel_id=1, source_target_pairs={{0,0},{8,24},{1,1},{9,25},{2,2},{10,26},{3,3},{11,27},{4,4},{12,28... | collective-permute-start | bytes 7077896 | tf_op jit(solution)/shard_map/ppermute | solution.py:20
  142.2 5.4 fusion.114
  147.7 8.5 %convolution_convert_fusion.13 = bf16[1024,768]{0,1:T(8,128)(2,1)} fusion(bf16[1536,768]{1,0:T(8,128)(2,1)} %collective-permute-done.10, bf16[1536,768]{1,0:T(8,128)(2,1)} %collective-permute-done.11, pred[]{:T(512)S(6)} %eq.26, f32[1024,1536]{1,0:T(8,128)S(1)} %fusion.114, f32[1536]{0:T(1024)S(1)} %add.363), kind=kOutput, calls=%fused_computation.180 | convolution fusion | flops 2433613824 | bytes 12589057 | tf_op jit(solution)/shard_map/dot_general | solution.py:188
  205.3 23.3 %collective-permute-start.19 = (bf16[1024,768]{0,1:T(8,128)(2,1)}, bf16[1024,768]{0,1:T(8,128)(2,1)}, u32[]{:S(2)}, u32[]{:S(2)}) collective-permute-start(bf16[1024,768]{0,1:T(8,128)(2,1)} %convolution_convert_fusion.6), channel_id=1, source_target_pairs={{0,16},{16,0},{1,17},{17,1},{2,18},{18,2},{3,19},{19,3},{4,20},{20... | collective-permute-start | bytes 4718600 | tf_op jit(solution)/shard_map/ppermute | solution.py:16
  241.5 5.6 fusion.115
  252.4 18.7 %collective-permute-start.47 = (bf16[768,768]{1,0:T(8,128)(2,1)S(1)}, bf16[768,768]{1,0:T(8,128)(2,1)S(1)}, u32[]{:S(2)}, u32[]{:S(2)}) collective-permute-start(bf16[768,768]{1,0:T(8,128)(2,1)S(1)} %get-tuple-element.109), channel_id=1, source_target_pairs={{0,16},{8,0},{16,24},{24,8},{1,17},{9,1},{17,25},{25,9},{2,18},{10... | collective-permute-start | bytes 3538952 | tf_op jit(solution)/shard_map/ppermute | solution.py:38
  271.1 7.3 convert_reduce_fusion
  285.9 24.4 %collective-permute-start.27 = (bf16[1024,768]{0,1:T(8,128)(2,1)S(1)}, bf16[1024,768]{0,1:T(8,128)(2,1)S(1)}, u32[]{:S(2)}, u32[]{:S(2)}) collective-permute-start(bf16[1024,768]{0,1:T(8,128)(2,1)S(1)} %convolution_convert_fusion.11), channel_id=1, source_target_pairs={{0,16},{16,0},{1,17},{17,1},{2,18},{18,2},{3,19},{19,3},{4,20},{20... | collective-permute-start | bytes 4718600 | tf_op jit(solution)/shard_map/ppermute | solution.py:16
  320.5 20.3 %collective-permute-done.45 = bf16[384,1536]{1,0:T(8,128)(2,1)S(1)} collective-permute-done((bf16[384,1536]{1,0:T(8,128)(2,1)S(1)}, bf16[384,1536]{1,0:T(8,128)(2,1)S(1)}, u32[]{:S(2)}, u32[]{:S(2)}) %collective-permute-start.45) | collective-permute-done | bytes 1179680 | tf_op jit(solution)/shard_map/ppermute | solution.py:38
  357.6 8.1 %multiply_reduce_fusion.3 = (f32[6,512]{1,0:T(8,128)S(1)}, f32[6,512,1024]{2,1,0:T(8,128)}) fusion(f32[6,512,1024]{2,1,0:T(8,128)S(1)} %bitcast.165, f32[6,512]{1,0:T(8,128)S(1)} %log_add_fusion.3, pred[512,1024]{1,0:T(8,128)(4,1)S(1)} %copy-done.11, bf16[512,6,64]{0,2,1:T(8,128)(2,1)} %bitcast.194, bf16[1024,6,64]{0,2,1:T(8,128)(2,1)} %copy-done.35), kind=kOutput, calls=%fused_computation.10 | convolution fusion | flops 415233024 | bytes 26894336 | tf_op jit(solution)/shard_map/qhd,khd->hqk/dot_general | solution.py:145
  365.8 5.5 convert_reduce_fusion.8
  371.2 9.5 %multiply_convert_fusion.3 = bf16[6,512,1024]{2,1,0:T(8,128)(2,1)} fusion(f32[6,512,1024]{2,1,0:T(8,128)} %get-tuple-element.160, f32[6,512,1024]{2,1,0:T(8,128)S(1)} %bitcast.165, f32[6,512]{1,0:T(8,128)S(1)} %get-tuple-element.159, f32[6,512]{1,0:T(8,128)S(1)} %log_add_fusion.3, pred[512,1024]{1,0:T(8,128)(4,1)S(1)} %copy-done.11), kind=kLoop, calls=%fused_computation.9 | loop fusion | flops 15728640 | bytes 32006144 | tf_op jit(solution)/shard_map/convert_element_type | solution.py:149
  387.5 6.7 multiply_reduce_fusion.2
  400.0 6.9 multiply_convert_fusion.2
  419.3 8.2 %collective-permute-start.40 = (bf16[384,1152]{1,0:T(8,128)(2,1)}, bf16[384,1152]{1,0:T(8,128)(2,1)}, u32[]{:S(2)}, u32[]{:S(2)}) collective-permute-start(bf16[384,1152]{1,0:T(8,128)(2,1)} %get-tuple-element.124), channel_id=1, source_target_pairs={{0,0},{8,16},{16,8},{24,24},{1,1},{9,17},{17,9},{25,25},{2,2},{10,... | collective-permute-start | bytes 2654216 | tf_op jit(solution)/shard_map/ppermute | solution.py:37
  432.4 11.7 %collective-permute-done.41 = bf16[384,1152]{1,0:T(8,128)(2,1)} collective-permute-done((bf16[384,1152]{1,0:T(8,128)(2,1)}, bf16[384,1152]{1,0:T(8,128)(2,1)}, u32[]{:S(2)}, u32[]{:S(2)}) %collective-permute-start.41) | collective-permute-done | bytes 884768 | tf_op jit(solution)/shard_map/ppermute | solution.py:38
  455.2 10.5 %convert_reduce_fusion.1 = (f32[1536]{0:T(1024)}, bf16[1024,1536]{1,0:T(8,128)(2,1)S(1)}) fusion(f32[1024,1536]{1,0:T(8,128)} %copy-done.105, f32[1536]{0:T(1024)S(1)} %copy-done.97, bf16[1024,768]{0,1:T(8,128)(2,1)S(1)} %get-tuple-element.89, bf16[1536,768]{1,0:T(8,128)(2,1)} %collective-permute-done.10, bf16[1536,768]{1,0:T(8,128)(2,1)} %collective-permute-done.11, ...), kind=kOutput, calls=%fused_computation.55 | convolution fusion | flops 2453273088 | bytes 15740929 | tf_op jit(solution)/shard_map/dot_general | solution.py:72
  468.9 5.6 convolution_convert_fusion.9
  476.1 10.4 %collective-permute-start.36 = (bf16[384,1536]{1,0:T(8,128)(2,1)}, bf16[384,1536]{1,0:T(8,128)(2,1)}, u32[]{:S(2)}, u32[]{:S(2)}) collective-permute-start(bf16[384,1536]{1,0:T(8,128)(2,1)} %get-tuple-element.114), channel_id=1, source_target_pairs={{0,0},{8,16},{16,8},{24,24},{1,1},{9,17},{17,9},{25,25},{2,2},{10,... | collective-permute-start | bytes 3538952 | tf_op jit(solution)/shard_map/ppermute | solution.py:37
  492.9 10.5 %collective-permute-start.38 = (bf16[768,768]{1,0:T(8,128)(2,1)}, bf16[768,768]{1,0:T(8,128)(2,1)}, u32[]{:S(2)}, u32[]{:S(2)}) collective-permute-start(bf16[768,768]{1,0:T(8,128)(2,1)} %get-tuple-element.112), channel_id=1, source_target_pairs={{0,0},{8,16},{16,8},{24,24},{1,1},{9,17},{17,9},{25,25},{2,2},{10,... | collective-permute-start | bytes 3538952 | tf_op jit(solution)/shard_map/ppermute | solution.py:37
  520.4 7.9 %fusion.8 = f32[6,64,1024]{2,1,0:T(8,128)} fusion(bf16[512,6,64]{0,2,1:T(8,128)(2,1)S(1)} %bitcast.196, f32[6,512,1024]{2,1,0:T(8,128)} %copy-done.3, f32[6,512]{1,0:T(8,128)S(1)} %copy-done.70, pred[512,1024]{1,0:T(8,128)(4,1)S(1)} %copy-done.15), kind=kOutput, calls=%fused_computation.36 | convolution fusion | flops 412090368 | bytes 15085568 | tf_op jit(solution)/shard_map/hqk,qhd->khd/dot_general | solution.py:156
  528.4 10.4 %multiply_reduce_fusion = (f32[6,512]{1,0:T(8,128)}, f32[6,512,1024]{2,1,0:T(8,128)}) fusion(f32[6,512,1024]{2,1,0:T(8,128)} %copy-done.3, f32[6,512]{1,0:T(8,128)S(1)} %copy-done.70, pred[512,1024]{1,0:T(8,128)(4,1)S(1)} %copy-done.15, bf16[512,6,64]{0,2,1:T(8,128)(2,1)S(1)} %bitcast.197, bf16[1024,6,64]{0,2,1:T(8,128)(2,1)S(1)} %copy-done.34), kind=kOutput, calls=%fused_computation.1 | convolution fusion | flops 415233024 | bytes 26894336 | tf_op jit(solution)/shard_map/qhd,khd->hqk/dot_general | solution.py:145
  538.8 7.9 %multiply_reduce_fusion.1 = (f32[6,512]{1,0:T(8,128)}, f32[6,512,1024]{2,1,0:T(8,128)}) fusion(f32[6,512,1024]{2,1,0:T(8,128)S(1)} %bitcast.169, f32[6,512]{1,0:T(8,128)S(1)} %copy-done.69, pred[512,1024]{1,0:T(8,128)(4,1)S(1)} %copy-done.12, bf16[512,6,64]{0,2,1:T(8,128)(2,1)S(1)} %bitcast.192, bf16[1024,6,64]{0,2,1:T(8,128)(2,1)S(1)} %copy-done.34), kind=kOutput, calls=%fused_computation.4 | convolution fusion | flops 415233024 | bytes 26894336 | tf_op jit(solution)/shard_map/qhd,khd->hqk/dot_general | solution.py:145
  546.7 16.8 %multiply_convert_fusion = (bf16[6,512,1024]{2,1,0:T(8,128)(2,1)S(1)}, bf16[6,512,1024]{2,1,0:T(8,128)(2,1)}) fusion(f32[6,512,1024]{2,1,0:T(8,128)} %get-tuple-element.166, f32[6,512,1024]{2,1,0:T(8,128)} %copy-done.3, f32[6,512]{1,0:T(8,128)} %get-tuple-element.165, f32[6,512]{1,0:T(8,128)} %log_add_fusion, pred[512,1024]{1,0:T(8,128)(4,1)} %copy-done.13, ...), kind=kLoop, calls=%fused_computation | loop fusion | flops 31457280 | bytes 64012288 | tf_op jit(solution)/shard_map/convert_element_type | solution.py:149
  581.2 8.5 %collective-permute-start.32 = (bf16[384,1152]{1,0:T(8,128)(2,1)}, bf16[384,1152]{1,0:T(8,128)(2,1)}, u32[]{:S(2)}, u32[]{:S(2)}) collective-permute-start(bf16[384,1152]{1,0:T(8,128)(2,1)} %get-tuple-element.126), channel_id=1, source_target_pairs={{0,0},{8,16},{16,8},{24,24},{1,1},{9,17},{17,9},{25,25},{2,2},{10,... | collective-permute-start | bytes 2654216 | tf_op jit(solution)/shard_map/ppermute | solution.py:37
  603.6 7.2 collective-permute-done.35
  625.8 40.8 %psum.68 = bf16[2,9,768]{2,1,0:T(8,128)(2,1)S(1)} all-reduce(bf16[2,9,768]{2,1,0:T(8,128)(2,1)S(1)} %add_convert_fusion.18), channel_id=1, replica_groups=mesh['section'=2,'tensor'=2,'dp'=8] {'dp'}, use_global_device_ids=true, to_apply=%region_51.52 | all-reduce | flops 13824 | bytes 55296 | tf_op jit(solution)/shard_map/psum | solution.py:308
  672.5 85.0 %all-reduce.5.cloned.1.call-done = (bf16[384,1152]{1,0:T(8,128)(2,1)}, bf16[192,768]{1,0:T(8,128)(2,1)}, bf16[384,1536]{1,0:T(8,128)(2,1)}, bf16[768,768]{1,0:T(8,128)(2,1)}) async-done(((bf16[384,1152]{1,0:T(8,128)(2,1)}, bf16[192,768]{1,0:T(8,128)(2,1)}, bf16[384,1536]{1,0:T(8,128)(2,1)}, bf16[768,768]{1,0:T(8,128)(2,1)}), (bf16[384,1152]{1,0:T(8,128)(2,1)}, bf16[192,768]{1,0:T(8,128)(2,1)}, ...) | async-done | bytes 3538960 | tf_op jit(solution)/shard_map/psum | solution.py:308
  (538 shorter events, 312.6 us)
Async XLA Ops:
  7.2 607.9 %all-reduce.7.cloned.1.call-start = ((), (), s32[]{:S(2)}) async-start(), calls=%async_computation.1 | async-start | bytes 7077888 | tf_op jit(solution)/shard_map/psum | solution.py:311
  10.1 31.4 %collective-permute-start.2 = (bf16[9,768]{1,0:T(8,128)(2,1)S(1)}, bf16[9,768]{1,0:T(8,128)(2,1)S(1)}, u32[]{:S(2)}, u32[]{:S(2)}) collective-permute-start(bf16[9,768]{1,0:T(8,128)(2,1)S(1)} %reshape.481), channel_id=1, source_target_pairs={{0,8},{8,16},{1,9},{9,17},{2,10},{10,18},{3,11},{11,19},{4,12},{12... | collective-permute-start | bytes 41480 | tf_op jit(solution)/shard_map/ppermute | solution.py:21
  15.0 31.3 %collective-permute-start.1 = (bf16[9,768]{1,0:T(8,128)(2,1)S(1)}, bf16[9,768]{1,0:T(8,128)(2,1)S(1)}, u32[]{:S(2)}, u32[]{:S(2)}) collective-permute-start(bf16[9,768]{1,0:T(8,128)(2,1)S(1)} %reshape.481), channel_id=1, source_target_pairs={{0,0},{8,24},{1,1},{9,25},{2,2},{10,26},{3,3},{11,27},{4,4},{12,28... | collective-permute-start | bytes 41480 | tf_op jit(solution)/shard_map/ppermute | solution.py:20
  19.5 42.3 %collective-permute-start.4 = (bf16[768,1152]{0,1:T(8,128)(2,1)}, bf16[768,1152]{0,1:T(8,128)(2,1)}, u32[]{:S(2)}, u32[]{:S(2)}) collective-permute-start(bf16[768,1152]{0,1:T(8,128)(2,1)} %bitcast.2), channel_id=1, source_target_pairs={{0,8},{8,16},{1,9},{9,17},{2,10},{10,18},{3,11},{11,19},{4,12},{12... | collective-permute-start | bytes 5308424 | tf_op jit(solution)/shard_map/ppermute | solution.py:21
  23.3 38.5 %collective-permute-start.3 = (bf16[768,1152]{0,1:T(8,128)(2,1)}, bf16[768,1152]{0,1:T(8,128)(2,1)}, u32[]{:S(2)}, u32[]{:S(2)}) collective-permute-start(bf16[768,1152]{0,1:T(8,128)(2,1)} %bitcast.2), channel_id=1, source_target_pairs={{0,0},{8,24},{1,1},{9,25},{2,2},{10,26},{3,3},{11,27},{4,4},{12,28... | collective-permute-start | bytes 5308424 | tf_op jit(solution)/shard_map/ppermute | solution.py:20
  41.5 46.4 %collective-permute-start.6 = (bf16[384,768]{1,0:T(8,128)(2,1)}, bf16[384,768]{1,0:T(8,128)(2,1)}, u32[]{:S(2)}, u32[]{:S(2)}) collective-permute-start(bf16[384,768]{1,0:T(8,128)(2,1)} %bitcast.228), channel_id=1, source_target_pairs={{0,8},{8,16},{1,9},{9,17},{2,10},{10,18},{3,11},{11,19},{4,12},{12... | collective-permute-start | bytes 1769480 | tf_op jit(solution)/shard_map/ppermute | solution.py:21
  46.3 41.7 %collective-permute-start.5 = (bf16[384,768]{1,0:T(8,128)(2,1)}, bf16[384,768]{1,0:T(8,128)(2,1)}, u32[]{:S(2)}, u32[]{:S(2)}) collective-permute-start(bf16[384,768]{1,0:T(8,128)(2,1)} %bitcast.229), channel_id=1, source_target_pairs={{0,0},{8,24},{1,1},{9,25},{2,2},{10,26},{3,3},{11,27},{4,4},{12,28... | collective-permute-start | bytes 1769480 | tf_op jit(solution)/shard_map/ppermute | solution.py:20
  90.9 46.6 %collective-permute-start.7 = (bf16[1024,768]{0,1:T(8,128)(2,1)S(1)}, bf16[1024,768]{0,1:T(8,128)(2,1)S(1)}, u32[]{:S(2)}, u32[]{:S(2)}) collective-permute-start(bf16[1024,768]{0,1:T(8,128)(2,1)S(1)} %convolution_convert_fusion.7), channel_id=1, source_target_pairs={{0,16},{16,0},{1,17},{17,1},{2,18},{18,2},{3,19},{19,3},{4,20},{20... | collective-permute-start | bytes 4718600 | tf_op jit(solution)/shard_map/ppermute | solution.py:16
  91.0 51.2 %collective-permute-start.9 = (bf16[768,1536]{1,0:T(8,128)(2,1)}, bf16[768,1536]{1,0:T(8,128)(2,1)}, u32[]{:S(2)}, u32[]{:S(2)}) collective-permute-start(bf16[768,1536]{1,0:T(8,128)(2,1)} %bitcast.16), channel_id=1, source_target_pairs={{0,8},{8,16},{1,9},{9,17},{2,10},{10,18},{3,11},{11,19},{4,12},{12... | collective-permute-start | bytes 7077896 | tf_op jit(solution)/shard_map/ppermute | solution.py:21
  96.3 45.9 %collective-permute-start.8 = (bf16[768,1536]{1,0:T(8,128)(2,1)}, bf16[768,1536]{1,0:T(8,128)(2,1)}, u32[]{:S(2)}, u32[]{:S(2)}) collective-permute-start(bf16[768,1536]{1,0:T(8,128)(2,1)} %bitcast.16), channel_id=1, source_target_pairs={{0,0},{8,24},{1,1},{9,25},{2,2},{10,26},{3,3},{11,27},{4,4},{12,28... | collective-permute-start | bytes 7077896 | tf_op jit(solution)/shard_map/ppermute | solution.py:20
  115.6 32.0 %collective-permute-start.11 = (bf16[1536,768]{1,0:T(8,128)(2,1)}, bf16[1536,768]{1,0:T(8,128)(2,1)}, u32[]{:S(2)}, u32[]{:S(2)}) collective-permute-start(bf16[1536,768]{1,0:T(8,128)(2,1)} %bitcast.17), channel_id=1, source_target_pairs={{0,8},{8,16},{1,9},{9,17},{2,10},{10,18},{3,11},{11,19},{4,12},{12... | collective-permute-start | bytes 7077896 | tf_op jit(solution)/shard_map/ppermute | solution.py:21
  169.4 31.8 %collective-permute-start.18 = (bf16[384,768]{1,0:T(8,128)(2,1)}, bf16[384,768]{1,0:T(8,128)(2,1)}, u32[]{:S(2)}, u32[]{:S(2)}) collective-permute-start(bf16[384,768]{1,0:T(8,128)(2,1)} %bitcast.230), channel_id=1, source_target_pairs={{16,8},{24,16},{17,9},{25,17},{18,10},{26,18},{19,11},{27,19},{20,... | collective-permute-start | bytes 1769480 | tf_op jit(solution)/shard_map/ppermute | solution.py:21
  170.9 30.3 %collective-permute-start.17 = (bf16[384,768]{1,0:T(8,128)(2,1)}, bf16[384,768]{1,0:T(8,128)(2,1)}, u32[]{:S(2)}, u32[]{:S(2)}) collective-permute-start(bf16[384,768]{1,0:T(8,128)(2,1)} %bitcast.231), channel_id=1, source_target_pairs={{16,0},{24,24},{17,1},{25,25},{18,2},{26,26},{19,3},{27,27},{20,4}... | collective-permute-start | bytes 1769480 | tf_op jit(solution)/shard_map/ppermute | solution.py:20
  173.4 60.7 %collective-permute-start.26 = (bf16[512,768]{0,1:T(8,128)(2,1)}, bf16[512,768]{0,1:T(8,128)(2,1)}, u32[]{:S(2)}, u32[]{:S(2)}) collective-permute-start(bf16[512,768]{0,1:T(8,128)(2,1)} %select_bitcast_fusion.6), channel_id=1, source_target_pairs={{0,8},{8,0},{1,9},{9,1},{2,10},{10,2},{3,11},{11,3},{4,12},{12,4},... | collective-permute-start | bytes 2359304 | tf_op jit(solution)/shard_map/ppermute | solution.py:16
  205.3 32.6 %collective-permute-start.19 = (bf16[1024,768]{0,1:T(8,128)(2,1)}, bf16[1024,768]{0,1:T(8,128)(2,1)}, u32[]{:S(2)}, u32[]{:S(2)}) collective-permute-start(bf16[1024,768]{0,1:T(8,128)(2,1)} %convolution_convert_fusion.6), channel_id=1, source_target_pairs={{0,16},{16,0},{1,17},{17,1},{2,18},{18,2},{3,19},{19,3},{4,20},{20... | collective-permute-start | bytes 4718600 | tf_op jit(solution)/shard_map/ppermute | solution.py:16
  231.9 39.2 %collective-permute-start.23 = (bf16[1536,768]{1,0:T(8,128)(2,1)}, bf16[1536,768]{1,0:T(8,128)(2,1)}, u32[]{:S(2)}, u32[]{:S(2)}) collective-permute-start(bf16[1536,768]{1,0:T(8,128)(2,1)} %bitcast.17), channel_id=1, source_target_pairs={{16,8},{24,16},{17,9},{25,17},{18,10},{26,18},{19,11},{27,19},{20,... | collective-permute-start | bytes 7077896 | tf_op jit(solution)/shard_map/ppermute | solution.py:21
  234.1 37.0 %collective-permute-start.22 = (bf16[1536,768]{1,0:T(8,128)(2,1)}, bf16[1536,768]{1,0:T(8,128)(2,1)S(1)}, u32[]{:S(2)}, u32[]{:S(2)}) collective-permute-start(bf16[1536,768]{1,0:T(8,128)(2,1)} %bitcast.17), channel_id=1, source_target_pairs={{16,0},{24,24},{17,1},{25,25},{18,2},{26,26},{19,3},{27,27},{20,4}... | collective-permute-start | bytes 7077896 | tf_op jit(solution)/shard_map/ppermute | solution.py:20
  251.6 65.9 %collective-permute-start.46 = (bf16[768,768]{1,0:T(8,128)(2,1)S(1)}, bf16[768,768]{1,0:T(8,128)(2,1)S(1)}, u32[]{:S(2)}, u32[]{:S(2)}) collective-permute-start(bf16[768,768]{1,0:T(8,128)(2,1)S(1)} %get-tuple-element.108), channel_id=1, source_target_pairs={{0,0},{8,16},{16,8},{24,24},{1,1},{9,17},{17,9},{25,25},{2,2},{10,... | collective-permute-start | bytes 3538952 | tf_op jit(solution)/shard_map/ppermute | solution.py:37
  252.4 66.8 %collective-permute-start.47 = (bf16[768,768]{1,0:T(8,128)(2,1)S(1)}, bf16[768,768]{1,0:T(8,128)(2,1)S(1)}, u32[]{:S(2)}, u32[]{:S(2)}) collective-permute-start(bf16[768,768]{1,0:T(8,128)(2,1)S(1)} %get-tuple-element.109), channel_id=1, source_target_pairs={{0,16},{8,0},{16,24},{24,8},{1,17},{9,1},{17,25},{25,9},{2,18},{10... | collective-permute-start | bytes 3538952 | tf_op jit(solution)/shard_map/ppermute | solution.py:38
  285.9 56.2 %collective-permute-start.27 = (bf16[1024,768]{0,1:T(8,128)(2,1)S(1)}, bf16[1024,768]{0,1:T(8,128)(2,1)S(1)}, u32[]{:S(2)}, u32[]{:S(2)}) collective-permute-start(bf16[1024,768]{0,1:T(8,128)(2,1)S(1)} %convolution_convert_fusion.11), channel_id=1, source_target_pairs={{0,16},{16,0},{1,17},{17,1},{2,18},{18,2},{3,19},{19,3},{4,20},{20... | collective-permute-start | bytes 4718600 | tf_op jit(solution)/shard_map/ppermute | solution.py:16
  311.2 29.6 %collective-permute-start.45 = (bf16[384,1536]{1,0:T(8,128)(2,1)S(1)}, bf16[384,1536]{1,0:T(8,128)(2,1)S(1)}, u32[]{:S(2)}, u32[]{:S(2)}) collective-permute-start(bf16[384,1536]{1,0:T(8,128)(2,1)S(1)} %get-tuple-element.111), channel_id=1, source_target_pairs={{0,16},{8,0},{16,24},{24,8},{1,17},{9,1},{17,25},{25,9},{2,18},{10... | collective-permute-start | bytes 3538952 | tf_op jit(solution)/shard_map/ppermute | solution.py:38
  317.5 76.7 %collective-permute-start.24 = (bf16[1024,768]{0,1:T(8,128)(2,1)}, bf16[1024,768]{0,1:T(8,128)(2,1)}, u32[]{:S(2)}, u32[]{:S(2)}) collective-permute-start(bf16[1024,768]{0,1:T(8,128)(2,1)} %convolution_convert_fusion.12), channel_id=1, source_target_pairs={{0,16},{16,0},{1,17},{17,1},{2,18},{18,2},{3,19},{19,3},{4,20},{20... | collective-permute-start | bytes 4718600 | tf_op jit(solution)/shard_map/ppermute | solution.py:16
  351.8 75.7 %collective-permute-start.42 = (bf16[192,768]{1,0:T(8,128)(2,1)}, bf16[192,768]{1,0:T(8,128)(2,1)S(1)}, u32[]{:S(2)}, u32[]{:S(2)}) collective-permute-start(bf16[192,768]{1,0:T(8,128)(2,1)} %get-tuple-element.143), channel_id=1, source_target_pairs={{0,0},{8,16},{16,8},{24,24},{1,1},{9,17},{17,9},{25,25},{2,2},{10,... | collective-permute-start | bytes 884744 | tf_op jit(solution)/shard_map/ppermute | solution.py:37
  353.4 74.2 %collective-permute-start.43 = (bf16[192,768]{1,0:T(8,128)(2,1)}, bf16[192,768]{1,0:T(8,128)(2,1)}, u32[]{:S(2)}, u32[]{:S(2)}) collective-permute-start(bf16[192,768]{1,0:T(8,128)(2,1)} %get-tuple-element.144), channel_id=1, source_target_pairs={{0,16},{8,0},{16,24},{24,8},{1,17},{9,1},{17,25},{25,9},{2,18},{10... | collective-permute-start | bytes 884744 | tf_op jit(solution)/shard_map/ppermute | solution.py:38
  398.0 31.4 %collective-permute-start.25 = (bf16[512,768]{0,1:T(8,128)(2,1)}, bf16[512,768]{0,1:T(8,128)(2,1)}, u32[]{:S(2)}, u32[]{:S(2)}) collective-permute-start(bf16[512,768]{0,1:T(8,128)(2,1)} %broadcast_select_fusion.42), channel_id=1, source_target_pairs={{0,8},{8,0},{1,9},{9,1},{2,10},{10,2},{3,11},{11,3},{4,12},{12,4},... | collective-permute-start | bytes 2359304 | tf_op jit(solution)/shard_map/ppermute | solution.py:16
  417.8 29.4 %collective-permute-start.28 = (bf16[1024,768]{0,1:T(8,128)(2,1)}, bf16[1024,768]{0,1:T(8,128)(2,1)}, u32[]{:S(2)}, u32[]{:S(2)}) collective-permute-start(bf16[1024,768]{0,1:T(8,128)(2,1)} %convolution_convert_fusion.10), channel_id=1, source_target_pairs={{0,16},{16,0},{1,17},{17,1},{2,18},{18,2},{3,19},{19,3},{4,20},{20... | collective-permute-start | bytes 4718600 | tf_op jit(solution)/shard_map/ppermute | solution.py:16
  446.7 310.8 %all-reduce.5.cloned.1.call-start = ((), (), s32[]{:S(2)}) async-start(), calls=%async_computation | async-start | bytes 7077888 | tf_op jit(solution)/shard_map/psum | solution.py:308
  474.6 35.6 %collective-permute-start.29 = (bf16[1024,768]{0,1:T(8,128)(2,1)}, bf16[1024,768]{0,1:T(8,128)(2,1)}, u32[]{:S(2)}, u32[]{:S(2)}) collective-permute-start(bf16[1024,768]{0,1:T(8,128)(2,1)} %convolution_convert_fusion.9), channel_id=1, source_target_pairs={{0,16},{16,0},{1,17},{17,1},{2,18},{18,2},{3,19},{19,3},{4,20},{20... | collective-permute-start | bytes 4718600 | tf_op jit(solution)/shard_map/ppermute | solution.py:16
  492.9 103.7 %collective-permute-start.38 = (bf16[768,768]{1,0:T(8,128)(2,1)}, bf16[768,768]{1,0:T(8,128)(2,1)}, u32[]{:S(2)}, u32[]{:S(2)}) collective-permute-start(bf16[768,768]{1,0:T(8,128)(2,1)} %get-tuple-element.112), channel_id=1, source_target_pairs={{0,0},{8,16},{16,8},{24,24},{1,1},{9,17},{17,9},{25,25},{2,2},{10,... | collective-permute-start | bytes 3538952 | tf_op jit(solution)/shard_map/ppermute | solution.py:37
  503.4 94.8 %collective-permute-start.39 = (bf16[768,768]{1,0:T(8,128)(2,1)}, bf16[768,768]{1,0:T(8,128)(2,1)}, u32[]{:S(2)}, u32[]{:S(2)}) collective-permute-start(bf16[768,768]{1,0:T(8,128)(2,1)} %get-tuple-element.113), channel_id=1, source_target_pairs={{0,16},{8,0},{16,24},{24,8},{1,17},{9,1},{17,25},{25,9},{2,18},{10... | collective-permute-start | bytes 3538952 | tf_op jit(solution)/shard_map/ppermute | solution.py:38
  581.2 31.4 %collective-permute-start.32 = (bf16[384,1152]{1,0:T(8,128)(2,1)}, bf16[384,1152]{1,0:T(8,128)(2,1)}, u32[]{:S(2)}, u32[]{:S(2)}) collective-permute-start(bf16[384,1152]{1,0:T(8,128)(2,1)} %get-tuple-element.126), channel_id=1, source_target_pairs={{0,0},{8,16},{16,8},{24,24},{1,1},{9,17},{17,9},{25,25},{2,2},{10,... | collective-permute-start | bytes 2654216 | tf_op jit(solution)/shard_map/ppermute | solution.py:37
  623.7 45.4 %collective-permute-start.31 = (bf16[512,768]{0,1:T(8,128)(2,1)S(1)}, bf16[512,768]{0,1:T(8,128)(2,1)S(1)}, u32[]{:S(2)}, u32[]{:S(2)}) collective-permute-start(bf16[512,768]{0,1:T(8,128)(2,1)S(1)} %broadcast_select_fusion.40), channel_id=1, source_target_pairs={{0,8},{8,0},{1,9},{9,1},{2,10},{10,2},{3,11},{11,3},{4,12},{12,4},... | collective-permute-start | bytes 2359304 | tf_op jit(solution)/shard_map/ppermute | solution.py:16
  (141 other events, 1637.5 us)
Sparse Core Ops, SparseCore 0:
  446.8 140.7 all-reduce.6
  615.2 142.1 all-reduce.4
